TPU v7x, 32 devices: a whole 2x2x4 slice. The times are simulated.
32 devices in a mesh: lat: 4 (over y, core), lon: 8 (over z, x).
Axes of the slice: x: 2, y: 2, z: 4, core: 2. Of those that a mesh axis runs over, the one named last changes fastest.
Arguments:
- latent: bfloat16 [8, 96, 640], P('lat', 'lon'), may hold values from -6 to 6
- lon_filter: bfloat16 [9, 96], replicated, may hold values from -0.625 to 0.625
- mix_weight: bfloat16 [9, 640, 20], P(None, 'lon'), may hold values from -1.25 to 1.25
- band_weight: bfloat16 [9, 8, 3], P(None, 'lat'), may hold values from -1.25 to 1.25
- offsets: int32 [8], P('lat'), may hold values from -2 to 7, as said below
- w_up: bfloat16 [640, 1280], replicated, may hold values from -0.25 to 0.25
- w_down: bfloat16 [1280, 640], replicated, may hold values from -0.15625 to 0.15625
Outputs:
- result: bfloat16 [8, 96, 640], P('lat', 'lon')
Inputs may be any that keep to these rules, and one draw needn't show every extreme that they name: offsets[i] - i lies between -2 and 0, so a band's rows lie within 2 rows of its output row; in every aligned block of 2 rows the first row's band starts 2 rows below it and the last row's band ends 2 rows above it.
All inputs are finite; a program needn't handle non-finite values.
Results may differ from a plain program's by a relative error of at most 0.0095.
Values may be sent and summed in bfloat16 or wider, within the bound.
No kernel may reach another device: no remote copies, remote signals or barrier semaphores. Data moves between devices by JAX's collectives and lax.ppermute only.
A program may use at most 128 MiB of HBM per device.

v0:
```python
import functools

import jax
import jax.numpy as jnp
from jax import lax
from jax.experimental import pallas as pl
from jax.experimental.pallas import tpu as pltpu
from jax.sharding import PartitionSpec as P

F32 = jnp.float32
BF16 = jnp.bfloat16
LANES = 128
SUBLANES = 8


def up_to(size, step):
    return -(-size // step) * step


def column_and_side():
    place = lax.axis_index("lon")
    return place // 2, place % 2


def message_rows(block):
    tiles = block // LANES
    return up_to(3 * SUBLANES * tiles + (SUBLANES if block % LANES else 0), 2 * SUBLANES)


def lanes_of(block):
    return up_to(block, LANES)


def fold(points, block):
    whole, rest = divmod(block, LANES)
    parts = [points[:, tile * LANES : (tile + 1) * LANES] for tile in range(whole)]
    if rest:
        odd = points[:, whole * LANES : (whole + 1) * LANES]
        kept = lax.broadcasted_iota(jnp.int32, (SUBLANES, LANES), 1) < rest
        shared = None
        for third in range(3):
            piece = jnp.where(kept, odd[third * SUBLANES : (third + 1) * SUBLANES], 0.0)
            piece = pltpu.roll(piece, third * rest, 1) if third else piece
            shared = piece if shared is None else shared + piece
        parts.append(shared)
    filled = sum(part.shape[0] for part in parts)
    if message_rows(block) > filled:
        parts.append(jnp.zeros((message_rows(block) - filled, LANES), F32))
    return jnp.concatenate(parts, axis=0).astype(BF16)


def unfold(message, block):
    whole, rest = divmod(block, LANES)
    groups = []
    for third in range(3):
        first = third * SUBLANES
        parts = [
            message[tile * 3 * SUBLANES + first : tile * 3 * SUBLANES + first + SUBLANES]
            for tile in range(whole)
        ]
        if rest:
            odd = message[whole * 3 * SUBLANES : whole * 3 * SUBLANES + SUBLANES]
            parts.append(pltpu.roll(odd, LANES - third * rest, 1) if third else odd)
        groups.append(jnp.concatenate(parts, axis=1) if len(parts) > 1 else parts[0])
    return groups


def group_points(latent_ref, points):
    width, rows, _ = latent_ref.shape
    rest = width - SUBLANES
    for row in range(rows):
        points[row * SUBLANES : (row + 1) * SUBLANES] = latent_ref[:SUBLANES, row, :].astype(F32)
        at = rows * SUBLANES + row * rest
        points[at : at + rest] = latent_ref[SUBLANES:, row, :].astype(F32)


def pack_kernel(latent_ref, *refs):
    *out_refs, points, stage = refs
    columns = len(out_refs)
    chans = latent_ref.shape[2]
    block = chans // columns
    column, _ = column_and_side()
    group_points(latent_ref, points)
    own = points[...]
    for target in range(columns):
        turned = pltpu.roll(own, chans - target * block, 1) if target else own
        stage[target] = fold(turned[:, : lanes_of(block)], block)
    for apart in range(columns):
        out_refs[apart][...] = stage[column ^ apart]


def column_kernel(order, *refs):
    *in_refs, out_ref = refs
    column, _ = column_and_side()
    for apart, ref in zip(order, in_refs):
        out_ref[column ^ apart] = ref[...]


def tables_kernel(width, filter_ref, band_ref, table_ref, first):
    bases, lons = filter_ref.shape
    taps, rows, _ = band_ref.shape
    step, places = first.shape[1:]
    columns = places // (2 * step)
    _, side = column_and_side()
    lat = lax.axis_index("lat")
    below = (lat > 0).astype(F32)
    above = (lat < lax.axis_size("lat") - 1).astype(F32)
    inside = [[below, below, 1.0], [1.0, above, above]]
    profile = filter_ref[...]
    band = band_ref[...].astype(F32)
    source = lax.broadcasted_iota(jnp.int32, (lons, places), 0)
    place = lax.broadcasted_iota(jnp.int32, (lons, places), 1)
    within = place % step
    apart = source + (place // step) * width + within + (lons - side * width)
    for _ in range(3):
        apart = jnp.where(apart >= lons, apart - lons, apart)
    apart = jnp.where(within < width, apart, -1)
    first[...] = jnp.zeros_like(first)
    for lon in range(width):
        pick = (apart == lon).astype(F32).astype(BF16)
        first[:, lon, :] = jnp.dot(profile, pick, preferred_element_type=F32)
    for basis in range(bases):
        circle = first[basis]
        for column in range(columns):
            turned = pltpu.roll(circle, column * 2 * step, 1) if column else circle
            at = (basis * columns + column) * step
            for row in range(rows):
                for tap in range(taps):
                    weight = band[tap, row : row + 1, basis : basis + 1] * inside[row][tap]
                    table_ref[row, at : at + step, tap * places : (tap + 1) * places] = (
                        weight * turned
                    ).astype(BF16)


def squares_kernel(own_ref, mate_ref, squares_ref, padded):
    bases, group, half = own_ref.shape
    lanes = squares_ref.shape[1]
    _, side = column_and_side()
    first = side == 0
    own = own_ref[...].astype(F32)
    mate = mate_ref[...].astype(F32)
    padded[...] = jnp.zeros_like(padded)
    padded[0, :, :group, :half] = jnp.where(first, own, mate)
    padded[1, :, :group, :half] = jnp.where(first, mate, own)
    members = padded.shape[2]
    into = lax.broadcasted_iota(jnp.int32, (lanes, members), 0)
    member = lax.broadcasted_iota(jnp.int32, (lanes, members), 1)
    repeat = (into % group == member).astype(F32).astype(BF16)
    row = lax.broadcasted_iota(jnp.int32, (lanes, lanes), 0)
    column = lax.broadcasted_iota(jnp.int32, (lanes, lanes), 1)
    same = (row // group == column // group) & (row < 2 * half) & (column < 2 * half)
    for basis in range(bases):
        weights = padded[0, basis] + pltpu.roll(padded[1, basis], half, 1)
        repeated = jnp.dot(repeat, weights.astype(BF16), preferred_element_type=F32)
        squares_ref[basis * lanes : (basis + 1) * lanes] = jnp.where(same, repeated, 0.0).astype(
            BF16
        )


def conv_kernel(block, width, *refs):
    odd_mate, odd_own, even_mate, mate, even_own, home = refs[:6]
    (table_ref, squares_ref), refs = refs[6:8], refs[8:]
    sources = ((home, mate), (even_own, even_mate), (odd_own, odd_mate))
    *out_refs, field, spread, stage = refs
    columns = len(out_refs)
    lanes = squares_ref.shape[1]
    bases = squares_ref.shape[0] // lanes
    rows, _, inner = table_ref.shape
    places = inner // 3
    step = places // (2 * columns)
    half = places // 2
    rest = width - SUBLANES
    column, side = column_and_side()
    odd = lax.axis_index("lat") % 2 == 1
    for at in range(2 * columns):
        here = side == at % 2
        own, even, other = (
            jnp.where(here, near[at // 2].astype(F32), far[at // 2].astype(F32))
            for near, far in sources
        )
        low = jnp.where(odd, even, other)
        high = jnp.where(odd, other, even)
        read = []
        for message in (low, own, high):
            groups = unfold(message, block)
            for row in range(rows):
                last = pltpu.roll(groups[2], SUBLANES - row * rest, 0) if row else groups[2]
                read.append(jnp.concatenate([groups[row], last], axis=0).astype(BF16))
        for row in range(rows):
            for tap in range(3):
                first = tap * places + at * step
                field[row, first : first + step] = read[row * 3 + tap]
    for row in range(rows):
        over = jnp.dot(table_ref[row], field[row], preferred_element_type=F32).astype(BF16)
        for basis in range(bases):
            spread[row * half : (row + 1) * half, basis * lanes : (basis + 1) * lanes] = over[
                basis * half : (basis + 1) * half
            ]
    mixed = jnp.dot(spread[...], squares_ref[...], preferred_element_type=F32)
    upper = lax.broadcasted_iota(jnp.int32, (SUBLANES, lanes), 0) < rest
    for target in range(columns):
        top = mixed[target * step : (target + 1) * step]
        bottom = mixed[half + target * step : half + (target + 1) * step]
        last = jnp.where(upper, top[SUBLANES:], pltpu.roll(bottom[SUBLANES:], rest, 0))
        points = jnp.concatenate([top[:SUBLANES], bottom[:SUBLANES], last], axis=0)
        stage[target] = fold(points, block)
    for apart in range(columns):
        out_refs[apart][...] = stage[column ^ apart]


def tail_kernel(order, *refs):
    columns = len(order)
    back_refs = refs[:columns]
    latent_ref, up_ref, down_ref, out_ref, points, stage = refs[columns:]
    width, rows, chans = latent_ref.shape
    rest = width - SUBLANES
    block = chans // columns
    lanes = lanes_of(block)
    column, _ = column_and_side()
    for apart, ref in zip(order, back_refs):
        stage[column ^ apart] = ref[...]
    group_points(latent_ref, points)
    kept = lax.broadcasted_iota(jnp.int32, (3 * SUBLANES, lanes), 1) < block
    convolved = None
    for target in range(columns):
        piece = jnp.concatenate(unfold(stage[target].astype(F32), block), axis=0)
        piece = jnp.where(kept, piece, 0.0)
        if chans > lanes:
            gap = jnp.zeros((3 * SUBLANES, chans - lanes), F32)
            piece = jnp.concatenate([piece, gap], axis=1)
        piece = pltpu.roll(piece, target * block, 1) if target else piece
        convolved = piece if convolved is None else convolved + piece
    summed = (points[...] + convolved).astype(BF16).astype(F32)
    centred = summed - jnp.mean(summed, axis=1, keepdims=True)
    variance = jnp.mean(centred * centred, axis=1, keepdims=True)
    normed = (centred * lax.rsqrt(variance + 1e-05)).astype(BF16)
    hidden = jnp.dot(normed, up_ref[...], preferred_element_type=F32)
    hidden = (0.5 * hidden * (1.0 + lax.erf(hidden * 0.5**0.5))).astype(BF16)
    result = summed + jnp.dot(hidden, down_ref[...], preferred_element_type=F32)
    for row in range(rows):
        out_ref[:SUBLANES, row, :] = result[row * SUBLANES : (row + 1) * SUBLANES].astype(BF16)
        at = rows * SUBLANES + row * rest
        out_ref[SUBLANES:, row, :] = result[at : at + rest].astype(BF16)


VMEM = pl.BlockSpec(memory_space=pltpu.VMEM)


def call(kernel, name, out_shape, scratch, work, *operands):
    several = isinstance(out_shape, tuple)
    return pl.pallas_call(
        kernel,
        out_shape=out_shape,
        in_specs=[VMEM] * len(operands),
        out_specs=(VMEM,) * len(out_shape) if several else VMEM,
        scratch_shapes=scratch,
        compiler_params=pltpu.CompilerParams(vmem_limit_bytes=24 * 2**20),
        cost_estimate=pl.CostEstimate(flops=work, bytes_accessed=10**6, transcendentals=0),
        name=name,
    )(*operands)


def over_columns(messages, count):
    arrived = {0: messages[0]}
    for apart in reversed(range(1, count // 2)):
        pairs = [(i, ((i // 2) ^ apart) * 2 + i % 2) for i in range(count)]
        arrived[apart] = lax.ppermute(messages[apart], "lon", pairs)
    return arrived


def over_sides(block, count):
    return lax.ppermute(block, "lon", [(i, i ^ 1) for i in range(count)])


def around(block, count):
    rows = lax.axis_size("lat")
    lat_even = [i ^ 1 for i in range(rows)]
    lat_odd = [((i - 1) ^ 1) + 1 if i else rows - 1 for i in range(rows)]
    lat_odd[rows - 1] = 0
    lat_self = list(range(rows))

    def swap(lat_of, other_side):
        pairs = [
            (lat * count + lon, lat_of[lat] * count + (lon ^ other_side))
            for lat in range(rows)
            for lon in range(count)
        ]
        return lax.ppermute(block, ("lat", "lon"), pairs)

    odd_mate = swap(lat_odd, 1)
    even_mate = swap(lat_even, 1)
    odd_own = swap(lat_odd, 0)
    mate = swap(lat_self, 1)
    even_own = swap(lat_even, 0)
    return odd_mate, odd_own, even_mate, mate, even_own


def local(latent, lon_filter, mix_weight, band_weight, offsets, w_up, w_down):
    rows, width, chans = latent.shape
    bases, lons = lon_filter.shape
    half, group = mix_weight.shape[1:]
    taps = band_weight.shape[2]
    count = lons // width
    columns = count // 2
    block = 2 * half
    step = up_to(width, 2 * SUBLANES)
    places = count * step
    lanes = lanes_of(block)
    height = message_rows(block)
    assert rows == 2 and taps == 3 and columns & (columns - 1) == 0
    assert SUBLANES < width and rows * (width - SUBLANES) <= SUBLANES
    assert 3 * (block % LANES) <= LANES

    far_first = tuple(reversed(range(columns)))
    near_then_far = (1,) + tuple(reversed(range(2, columns))) + (0,)
    message = jax.ShapeDtypeStruct((height, LANES), BF16)
    messages = (message,) * columns
    stage = pltpu.VMEM((columns, height, LANES), BF16)
    points = pltpu.VMEM((3 * SUBLANES, chans), F32)
    lon_first = jnp.transpose(latent, (1, 0, 2))
    mix_own = jnp.transpose(mix_weight, (0, 2, 1))

    packed = call(pack_kernel, "pack", messages, [points, stage], 10**9, lon_first)
    arrived = over_columns(packed, count)
    mix_mate = over_sides(mix_own, count)
    table = call(
        functools.partial(tables_kernel, width),
        "tables",
        jax.ShapeDtypeStruct((rows, bases * places // 2, taps * places), BF16),
        [pltpu.VMEM((bases, step, places), F32)],
        10**9,
        lon_filter,
        jnp.transpose(band_weight, (2, 1, 0)),
    )
    squares = call(
        squares_kernel,
        "squares",
        jax.ShapeDtypeStruct((bases * lanes, lanes), BF16),
        [pltpu.VMEM((2, bases, up_to(group, 2 * SUBLANES), lanes), F32)],
        10**9,
        mix_own,
        mix_mate,
    )
    gathered = jax.ShapeDtypeStruct((columns, height, LANES), BF16)
    own_side = call(
        functools.partial(column_kernel, far_first),
        "join_columns",
        gathered,
        [],
        10**8,
        *[arrived[apart] for apart in far_first],
    )
    sources = around(own_side, count)
    mixed = call(
        functools.partial(conv_kernel, block, width),
        "conv",
        messages,
        [
            pltpu.VMEM((rows, taps * places, lanes), BF16),
            pltpu.VMEM((rows * places // 2, bases * lanes), BF16),
            stage,
        ],
        10**10,
        *sources,
        own_side,
        table,
        squares,
    )
    back = over_columns(mixed, count)
    result = call(
        functools.partial(tail_kernel, near_then_far),
        "tail",
        jax.ShapeDtypeStruct(lon_first.shape, BF16),
        [points, stage],
        10**9,
        *[back[apart] for apart in near_then_far],
        lon_first,
        w_up,
        w_down,
    )
    return jnp.transpose(result, (1, 0, 2))


def solution(mesh):
    return jax.shard_map(
        local,
        mesh=mesh,
        in_specs=(
            P("lat", "lon", None),
            P(),
            P(None, "lon", None),
            P(None, "lat", None),
            P("lat"),
            P(),
            P(),
        ),
        out_specs=P("lat", "lon", None),
        check_vma=False,
    )
```

profile of v0, /device:TPU:0, one launch (start us, length us, event | category | flops | bytes accessed | tf_op | source)
XLA Modules:
  0.0 26.5 jit_solution(51052655786232673)
XLA Ops:
  0.0 0.0 copy-start.3
  0.0 0.8 %copy-done.3 = bf16[2,12,640]{2,0,1:T(2,128)(2,1)S(1)} copy-done((bf16[2,12,640]{2,0,1:T(2,128)(2,1)S(1)}, bf16[2,12,640]{2,0,1:T(2,128)(2,1)}, u32[]{:S(2)}) %copy-start.3) | copy-done | bytes 30744
  0.8 0.0 copy-start.2
  0.8 0.0 copy-start.5
  0.8 0.0 copy-start.6
  0.8 0.2 pack.1
  0.9 5.1 %collective-permute-start = (bf16[32,128]{1,0:T(8,128)(2,1)S(1)}, bf16[32,128]{1,0:T(8,128)(2,1)S(1)}, u32[]{:S(2)}, u32[]{:S(2)}) collective-permute-start(bf16[32,128]{1,0:T(8,128)(2,1)S(1)} %get-tuple-element.13), channel_id=1, source_target_pairs={{0,6},{1,7},{2,4},{3,5},{4,2},{5,3},{6,0},{7,1},{8,14},{9,15},{10,... | collective-permute-start | bytes 24584 | tf_op jit(solution)/shard_map/ppermute | solution.py:267
  6.1 0.0 collective-permute-start.1
  6.1 0.6 %collective-permute-start.2 = (bf16[32,128]{1,0:T(8,128)(2,1)S(1)}, bf16[32,128]{1,0:T(8,128)(2,1)S(1)}, u32[]{:S(2)}, u32[]{:S(2)}) collective-permute-start(bf16[32,128]{1,0:T(8,128)(2,1)S(1)} %get-tuple-element.15), channel_id=1, source_target_pairs={{0,2},{1,3},{2,0},{3,1},{4,6},{5,7},{6,4},{7,5},{8,10},{9,11},{10,... | collective-permute-start | bytes 24584 | tf_op jit(solution)/shard_map/ppermute | solution.py:267
  6.7 0.0 copy-done.2
  6.7 1.6 %collective-permute-start.8 = (bf16[9,20,80]{2,1,0:T(8,128)(2,1)S(1)}, bf16[9,20,80]{2,1,0:T(8,128)(2,1)S(1)}, u32[]{:S(2)}, u32[]{:S(2)}) collective-permute-start(bf16[9,20,80]{2,1,0:T(8,128)(2,1)S(1)} %bitcast.4), channel_id=1, source_target_pairs={{0,1},{1,0},{2,3},{3,2},{4,5},{5,4},{6,7},{7,6},{8,9},{9,8},{10,11... | collective-permute-start | bytes 86408 | tf_op jit(solution)/shard_map/ppermute | solution.py:272
  8.3 0.0 copy-done.5
  8.3 0.0 copy-done.6
  8.3 0.4 %tables.1.refs_6_ = bf16[2,576,384]{2,1,0:T(8,128)(2,1)S(1)} custom-call(bf16[9,96]{1,0:T(8,128)(2,1)S(1)} %copy-done.5, bf16[3,2,9]{2,1,0:T(2,128)(2,1)S(1)} %bitcast.8), custom_call_target="tpu_custom_call" | custom-call | flops 1000000000 | bytes 1000000 | tf_op jit(solution)/shard_map/tables/pallas_call | solution.py:251
  8.7 0.0 collective-permute-done.refs_0_
  8.8 1.8 %collective-permute-done.1.refs_1_ = bf16[32,128]{1,0:T(8,128)(2,1)S(1)} collective-permute-done((bf16[32,128]{1,0:T(8,128)(2,1)S(1)}, bf16[32,128]{1,0:T(8,128)(2,1)S(1)}, u32[]{:S(2)}, u32[]{:S(2)}) %collective-permute-start.1) | collective-permute-done | bytes 8224 | tf_op jit(solution)/shard_map/ppermute | solution.py:267
  10.6 0.0 collective-permute-done.2.refs_2_
  10.6 0.5 %collective-permute-start.3 = (bf16[4,32,128]{2,1,0:T(8,128)(2,1)S(1)}, bf16[4,32,128]{2,1,0:T(8,128)(2,1)S(1)}, u32[]{:S(2)}, u32[]{:S(2)}) collective-permute-start(bf16[4,32,128]{2,1,0:T(8,128)(2,1)S(1)} %join_columns.1.refs_5_), channel_id=1, source_target_pairs={{0,25},{1,24},{2,27},{3,26},{4,29},{5,28},{6,31},{7,30},{8,17},{9,... | collective-permute-start | bytes 98312 | tf_op jit(solution)/shard_map/ppermute | solution.py:288
  11.1 2.2 %collective-permute-start.4 = (bf16[4,32,128]{2,1,0:T(8,128)(2,1)S(1)}, bf16[4,32,128]{2,1,0:T(8,128)(2,1)S(1)}, u32[]{:S(2)}, u32[]{:S(2)}) collective-permute-start(bf16[4,32,128]{2,1,0:T(8,128)(2,1)S(1)} %join_columns.1.refs_5_), channel_id=1, source_target_pairs={{0,24},{1,25},{2,26},{3,27},{4,28},{5,29},{6,30},{7,31},{8,16},{9,... | collective-permute-start | bytes 98312 | tf_op jit(solution)/shard_map/ppermute | solution.py:288
  13.4 0.1 collective-permute-start.5
  13.5 1.4 %collective-permute-start.6 = (bf16[4,32,128]{2,1,0:T(8,128)(2,1)S(1)}, bf16[4,32,128]{2,1,0:T(8,128)(2,1)S(1)}, u32[]{:S(2)}, u32[]{:S(2)}) collective-permute-start(bf16[4,32,128]{2,1,0:T(8,128)(2,1)S(1)} %join_columns.1.refs_5_), channel_id=1, source_target_pairs={{0,1},{1,0},{2,3},{3,2},{4,5},{5,4},{6,7},{7,6},{8,9},{9,8},{10,11... | collective-permute-start | bytes 98312 | tf_op jit(solution)/shard_map/ppermute | solution.py:288
  14.9 0.0 collective-permute-done.8.mate_ref
  14.9 0.3 %collective-permute-start.7 = (bf16[4,32,128]{2,1,0:T(8,128)(2,1)S(1)}, bf16[4,32,128]{2,1,0:T(8,128)(2,1)S(1)}, u32[]{:S(2)}, u32[]{:S(2)}) collective-permute-start(bf16[4,32,128]{2,1,0:T(8,128)(2,1)S(1)} %join_columns.1.refs_5_), channel_id=1, source_target_pairs={{0,8},{1,9},{2,10},{3,11},{4,12},{5,13},{6,14},{7,15},{8,0},{9,1},... | collective-permute-start | bytes 98312 | tf_op jit(solution)/shard_map/ppermute | solution.py:288
  15.2 0.5 %squares.1.refs_7_ = bf16[2304,256]{1,0:T(8,128)(2,1)S(1)} custom-call(bf16[9,20,80]{2,1,0:T(8,128)(2,1)S(1)} %bitcast.5, bf16[9,20,80]{2,1,0:T(8,128)(2,1)S(1)} %collective-permute-done.8.mate_ref), custom_call_target="tpu_custom_call" | custom-call | flops 1000000000 | bytes 1000000 | tf_op jit(solution)/shard_map/squares/pallas_call | solution.py:251
  15.8 0.0 copy-start
  15.8 0.0 copy-start.1
  15.8 0.0 copy-start.4
  15.8 0.0 collective-permute-done.3.refs_0_
  15.8 0.0 collective-permute-done.4.refs_1_
  15.8 1.1 %collective-permute-done.5.refs_2_ = bf16[4,32,128]{2,1,0:T(8,128)(2,1)S(1)} collective-permute-done((bf16[4,32,128]{2,1,0:T(8,128)(2,1)S(1)}, bf16[4,32,128]{2,1,0:T(8,128)(2,1)S(1)}, u32[]{:S(2)}, u32[]{:S(2)}) %collective-permute-start.5) | collective-permute-done | bytes 32800 | tf_op jit(solution)/shard_map/ppermute | solution.py:288
  17.0 0.8 %collective-permute-done.6.refs_3_ = bf16[4,32,128]{2,1,0:T(8,128)(2,1)S(1)} collective-permute-done((bf16[4,32,128]{2,1,0:T(8,128)(2,1)S(1)}, bf16[4,32,128]{2,1,0:T(8,128)(2,1)S(1)}, u32[]{:S(2)}, u32[]{:S(2)}) %collective-permute-start.6) | collective-permute-done | bytes 32800 | tf_op jit(solution)/shard_map/ppermute | solution.py:288
  17.7 0.0 collective-permute-done.7.refs_4_
  17.7 1.0 %conv.1 = (bf16[32,128]{1,0:T(8,128)(2,1)S(1)}, bf16[32,128]{1,0:T(8,128)(2,1)S(1)}, bf16[32,128]{1,0:T(8,128)(2,1)S(1)}, bf16[32,128]{1,0:T(8,128)(2,1)S(1)}) custom-call(bf16[4,32,128]{2,1,0:T(8,128)(2,1)S(1)} %collective-permute-done.3.refs_0_, bf16[4,32,128]{2,1,0:T(8,128)(2,1)S(1)} %collective-permute-done.4.refs_1_, ...), custom_call_target="tpu_custom_call" | custom-call | flops 10000000000 | bytes 1000000 | tf_op jit(solution)/shard_map/conv/pallas_call | solution.py:251
  18.8 1.5 %collective-permute-start.10 = (bf16[32,128]{1,0:T(8,128)(2,1)S(1)}, bf16[32,128]{1,0:T(8,128)(2,1)S(1)}, u32[]{:S(2)}, u32[]{:S(2)}) collective-permute-start(bf16[32,128]{1,0:T(8,128)(2,1)S(1)} %get-tuple-element.18), channel_id=1, source_target_pairs={{0,6},{1,7},{2,4},{3,5},{4,2},{5,3},{6,0},{7,1},{8,14},{9,15},{10,... | collective-permute-start | bytes 24584 | tf_op jit(solution)/shard_map/ppermute | solution.py:267
  20.3 0.6 %collective-permute-start.11 = (bf16[32,128]{1,0:T(8,128)(2,1)S(1)}, bf16[32,128]{1,0:T(8,128)(2,1)S(1)}, u32[]{:S(2)}, u32[]{:S(2)}) collective-permute-start(bf16[32,128]{1,0:T(8,128)(2,1)S(1)} %get-tuple-element.19), channel_id=1, source_target_pairs={{0,4},{1,5},{2,6},{3,7},{4,0},{5,1},{6,2},{7,3},{8,12},{9,13},{10,... | collective-permute-start | bytes 24584 | tf_op jit(solution)/shard_map/ppermute | solution.py:267
  20.9 2.4 %collective-permute-start.9 = (bf16[32,128]{1,0:T(8,128)(2,1)S(1)}, bf16[32,128]{1,0:T(8,128)(2,1)S(1)}, u32[]{:S(2)}, u32[]{:S(2)}) collective-permute-start(bf16[32,128]{1,0:T(8,128)(2,1)S(1)} %get-tuple-element.17), channel_id=1, source_target_pairs={{0,2},{1,3},{2,0},{3,1},{4,6},{5,7},{6,4},{7,5},{8,10},{9,11},{10,... | collective-permute-start | bytes 24584 | tf_op jit(solution)/shard_map/ppermute | solution.py:267
  23.2 1.1 %collective-permute-done.10.refs_1_ = bf16[32,128]{1,0:T(8,128)(2,1)S(1)} collective-permute-done((bf16[32,128]{1,0:T(8,128)(2,1)S(1)}, bf16[32,128]{1,0:T(8,128)(2,1)S(1)}, u32[]{:S(2)}, u32[]{:S(2)}) %collective-permute-start.10) | collective-permute-done | bytes 8224 | tf_op jit(solution)/shard_map/ppermute | solution.py:267
  24.3 0.5 %collective-permute-done.11.refs_2_ = bf16[32,128]{1,0:T(8,128)(2,1)S(1)} collective-permute-done((bf16[32,128]{1,0:T(8,128)(2,1)S(1)}, bf16[32,128]{1,0:T(8,128)(2,1)S(1)}, u32[]{:S(2)}, u32[]{:S(2)}) %collective-permute-start.11) | collective-permute-done | bytes 8224 | tf_op jit(solution)/shard_map/ppermute | solution.py:267
  24.8 0.1 collective-permute-done.9.refs_0_
  24.9 0.0 copy-done
  24.9 0.0 copy-done.1
  24.9 0.0 copy-done.4
  24.9 1.6 %tail.1 = bf16[12,2,640]{2,1,0:T(2,128)(2,1)} custom-call(bf16[32,128]{1,0:T(8,128)(2,1)S(1)} %collective-permute-done.9.refs_0_, bf16[32,128]{1,0:T(8,128)(2,1)S(1)} %collective-permute-done.10.refs_1_, bf16[32,128]{1,0:T(8,128)(2,1)S(1)} %collective-permute-done.11.refs_2_, bf16[32,128]{1,0:T(8,128)(2,1)S(1)} %get-tuple-element.20.refs_3_, ...), custom_call_target="tpu_custom_call" | custom-call | flops 1000000000 | bytes 1000000 | tf_op jit(solution)/shard_map/tail/pallas_call | solution.py:251
  (1 shorter events, 0.0 us)
Async XLA Ops:
  0.0 0.8 %copy-start.3 = (bf16[2,12,640]{2,0,1:T(2,128)(2,1)S(1)}, bf16[2,12,640]{2,0,1:T(2,128)(2,1)}, u32[]{:S(2)}) copy-start(bf16[2,12,640]{2,0,1:T(2,128)(2,1)} %param.7) | copy-start | bytes 92164
  0.8 5.9 %copy-start.2 = (bf16[9,80,20]{1,2,0:T(8,128)(2,1)S(1)}, bf16[9,80,20]{1,2,0:T(8,128)(2,1)}, u32[]{:S(2)}) copy-start(bf16[9,80,20]{1,2,0:T(8,128)(2,1)} %param.9) | copy-start | bytes 86404
  0.8 7.6 %copy-start.5 = (bf16[9,96]{1,0:T(8,128)(2,1)S(1)}, bf16[9,96]{1,0:T(8,128)(2,1)}, u32[]{:S(2)}) copy-start(bf16[9,96]{1,0:T(8,128)(2,1)} %filter_ref.1) | copy-start | bytes 5188
  0.8 7.6 %copy-start.6 = (bf16[9,2,3]{0,1,2:T(2,128)(2,1)S(1)}, bf16[9,2,3]{0,1,2:T(2,128)(2,1)}, u32[]{:S(2)}) copy-start(bf16[9,2,3]{0,1,2:T(2,128)(2,1)} %param.10) | copy-start | bytes 328
  0.9 7.8 %collective-permute-start = (bf16[32,128]{1,0:T(8,128)(2,1)S(1)}, bf16[32,128]{1,0:T(8,128)(2,1)S(1)}, u32[]{:S(2)}, u32[]{:S(2)}) collective-permute-start(bf16[32,128]{1,0:T(8,128)(2,1)S(1)} %get-tuple-element.13), channel_id=1, source_target_pairs={{0,6},{1,7},{2,4},{3,5},{4,2},{5,3},{6,0},{7,1},{8,14},{9,15},{10,... | collective-permute-start | bytes 24584 | tf_op jit(solution)/shard_map/ppermute | solution.py:267
  6.1 4.5 %collective-permute-start.1 = (bf16[32,128]{1,0:T(8,128)(2,1)S(1)}, bf16[32,128]{1,0:T(8,128)(2,1)S(1)}, u32[]{:S(2)}, u32[]{:S(2)}) collective-permute-start(bf16[32,128]{1,0:T(8,128)(2,1)S(1)} %get-tuple-element.14), channel_id=1, source_target_pairs={{0,4},{1,5},{2,6},{3,7},{4,0},{5,1},{6,2},{7,3},{8,12},{9,13},{10,... | collective-permute-start | bytes 24584 | tf_op jit(solution)/shard_map/ppermute | solution.py:267
  6.1 4.5 %collective-permute-start.2 = (bf16[32,128]{1,0:T(8,128)(2,1)S(1)}, bf16[32,128]{1,0:T(8,128)(2,1)S(1)}, u32[]{:S(2)}, u32[]{:S(2)}) collective-permute-start(bf16[32,128]{1,0:T(8,128)(2,1)S(1)} %get-tuple-element.15), channel_id=1, source_target_pairs={{0,2},{1,3},{2,0},{3,1},{4,6},{5,7},{6,4},{7,5},{8,10},{9,11},{10,... | collective-permute-start | bytes 24584 | tf_op jit(solution)/shard_map/ppermute | solution.py:267
  6.7 8.2 %collective-permute-start.8 = (bf16[9,20,80]{2,1,0:T(8,128)(2,1)S(1)}, bf16[9,20,80]{2,1,0:T(8,128)(2,1)S(1)}, u32[]{:S(2)}, u32[]{:S(2)}) collective-permute-start(bf16[9,20,80]{2,1,0:T(8,128)(2,1)S(1)} %bitcast.4), channel_id=1, source_target_pairs={{0,1},{1,0},{2,3},{3,2},{4,5},{5,4},{6,7},{7,6},{8,9},{9,8},{10,11... | collective-permute-start | bytes 86408 | tf_op jit(solution)/shard_map/ppermute | solution.py:272
  10.6 5.2 %collective-permute-start.3 = (bf16[4,32,128]{2,1,0:T(8,128)(2,1)S(1)}, bf16[4,32,128]{2,1,0:T(8,128)(2,1)S(1)}, u32[]{:S(2)}, u32[]{:S(2)}) collective-permute-start(bf16[4,32,128]{2,1,0:T(8,128)(2,1)S(1)} %join_columns.1.refs_5_), channel_id=1, source_target_pairs={{0,25},{1,24},{2,27},{3,26},{4,29},{5,28},{6,31},{7,30},{8,17},{9,... | collective-permute-start | bytes 98312 | tf_op jit(solution)/shard_map/ppermute | solution.py:288
  11.1 4.7 %collective-permute-start.4 = (bf16[4,32,128]{2,1,0:T(8,128)(2,1)S(1)}, bf16[4,32,128]{2,1,0:T(8,128)(2,1)S(1)}, u32[]{:S(2)}, u32[]{:S(2)}) collective-permute-start(bf16[4,32,128]{2,1,0:T(8,128)(2,1)S(1)} %join_columns.1.refs_5_), channel_id=1, source_target_pairs={{0,24},{1,25},{2,26},{3,27},{4,28},{5,29},{6,30},{7,31},{8,16},{9,... | collective-permute-start | bytes 98312 | tf_op jit(solution)/shard_map/ppermute | solution.py:288
  13.4 3.6 %collective-permute-start.5 = (bf16[4,32,128]{2,1,0:T(8,128)(2,1)S(1)}, bf16[4,32,128]{2,1,0:T(8,128)(2,1)S(1)}, u32[]{:S(2)}, u32[]{:S(2)}) collective-permute-start(bf16[4,32,128]{2,1,0:T(8,128)(2,1)S(1)} %join_columns.1.refs_5_), channel_id=1, source_target_pairs={{0,9},{1,8},{2,11},{3,10},{4,13},{5,12},{6,15},{7,14},{8,1},{9,0},... | collective-permute-start | bytes 98312 | tf_op jit(solution)/shard_map/ppermute | solution.py:288
  13.5 4.3 %collective-permute-start.6 = (bf16[4,32,128]{2,1,0:T(8,128)(2,1)S(1)}, bf16[4,32,128]{2,1,0:T(8,128)(2,1)S(1)}, u32[]{:S(2)}, u32[]{:S(2)}) collective-permute-start(bf16[4,32,128]{2,1,0:T(8,128)(2,1)S(1)} %join_columns.1.refs_5_), channel_id=1, source_target_pairs={{0,1},{1,0},{2,3},{3,2},{4,5},{5,4},{6,7},{7,6},{8,9},{9,8},{10,11... | collective-permute-start | bytes 98312 | tf_op jit(solution)/shard_map/ppermute | solution.py:288
  14.9 2.9 %collective-permute-start.7 = (bf16[4,32,128]{2,1,0:T(8,128)(2,1)S(1)}, bf16[4,32,128]{2,1,0:T(8,128)(2,1)S(1)}, u32[]{:S(2)}, u32[]{:S(2)}) collective-permute-start(bf16[4,32,128]{2,1,0:T(8,128)(2,1)S(1)} %join_columns.1.refs_5_), channel_id=1, source_target_pairs={{0,8},{1,9},{2,10},{3,11},{4,12},{5,13},{6,14},{7,15},{8,0},{9,1},... | collective-permute-start | bytes 98312 | tf_op jit(solution)/shard_map/ppermute | solution.py:288
  15.8 9.1 %copy-start = (bf16[640,1280]{1,0:T(8,128)(2,1)S(1)}, bf16[640,1280]{1,0:T(8,128)(2,1)}, u32[]{:S(2)}) copy-start(bf16[640,1280]{1,0:T(8,128)(2,1)} %refs_5_.1) | copy-start | bytes 4915204
  15.8 9.1 %copy-start.1 = (bf16[1280,640]{1,0:T(8,128)(2,1)S(1)}, bf16[1280,640]{1,0:T(8,128)(2,1)}, u32[]{:S(2)}) copy-start(bf16[1280,640]{1,0:T(8,128)(2,1)} %refs_6_.1) | copy-start | bytes 4915204
  15.8 9.1 %copy-start.4 = (bf16[2,12,640]{2,0,1:T(2,128)(2,1)S(1)}, bf16[2,12,640]{2,0,1:T(2,128)(2,1)}, u32[]{:S(2)}) copy-start(bf16[2,12,640]{2,0,1:T(2,128)(2,1)} %param.7) | copy-start | bytes 92164
  18.8 5.5 %collective-permute-start.10 = (bf16[32,128]{1,0:T(8,128)(2,1)S(1)}, bf16[32,128]{1,0:T(8,128)(2,1)S(1)}, u32[]{:S(2)}, u32[]{:S(2)}) collective-permute-start(bf16[32,128]{1,0:T(8,128)(2,1)S(1)} %get-tuple-element.18), channel_id=1, source_target_pairs={{0,6},{1,7},{2,4},{3,5},{4,2},{5,3},{6,0},{7,1},{8,14},{9,15},{10,... | collective-permute-start | bytes 24584 | tf_op jit(solution)/shard_map/ppermute | solution.py:267
  20.3 4.5 %collective-permute-start.11 = (bf16[32,128]{1,0:T(8,128)(2,1)S(1)}, bf16[32,128]{1,0:T(8,128)(2,1)S(1)}, u32[]{:S(2)}, u32[]{:S(2)}) collective-permute-start(bf16[32,128]{1,0:T(8,128)(2,1)S(1)} %get-tuple-element.19), channel_id=1, source_target_pairs={{0,4},{1,5},{2,6},{3,7},{4,0},{5,1},{6,2},{7,3},{8,12},{9,13},{10,... | collective-permute-start | bytes 24584 | tf_op jit(solution)/shard_map/ppermute | solution.py:267
  20.9 4.0 %collective-permute-start.9 = (bf16[32,128]{1,0:T(8,128)(2,1)S(1)}, bf16[32,128]{1,0:T(8,128)(2,1)S(1)}, u32[]{:S(2)}, u32[]{:S(2)}) collective-permute-start(bf16[32,128]{1,0:T(8,128)(2,1)S(1)} %get-tuple-element.17), channel_id=1, source_target_pairs={{0,2},{1,3},{2,0},{3,1},{4,6},{5,7},{6,4},{7,5},{8,10},{9,11},{10,... | collective-permute-start | bytes 24584 | tf_op jit(solution)/shard_map/ppermute | solution.py:267
where the time goes:
time: 26.7 us; the launch traced here: 26.5 us
  starting transfers between devices  16.4 us (61%)
  waiting for transfers between devices  5.42 us (20%)
  Pallas kernels  3.79 us (14%)
  local copies, waits for them, and re-layouts  0.78 us (3%)
    ppermute x6, starting transfers between devices, over_columns(): arrived[apart] = lax.ppermute(messages[apart], 'lon', pairs)  10.2 us
    ppermute x5, starting transfers between devices, swap(): return lax.ppermute(block, ('lat', 'lon'), pairs)  4.6 us
    pallas_call x6, Pallas kernels, call(): pl.pallas_call(kernel, out_shape=out_shape, in_specs=[VMEM] * len(operand...  3.79 us
    ppermute x6, waiting for transfers between devices, over_columns(): arrived[apart] = lax.ppermute(messages[apart], 'lon', pairs)  3.49 us
    ppermute x5, waiting for transfers between devices, swap(): return lax.ppermute(block, ('lat', 'lon'), pairs)  1.92 us
    ppermute x1, starting transfers between devices, over_sides(): return lax.ppermute(block, 'lon', [(i, i ^ 1) for i in range(count)])  1.63 us
    unnamed x14, local copies, waits for them, and re-layouts  0.78 us
  transfers between devices with their start and end apart: 12, of which 6 were waited for; matrix products, arithmetic and copies ran while one was open for 0% of the time, Pallas kernels for 4%

commit v1 on v0

--- a/solution.py
+++ b/solution.py
@@ -106,6 +106,7 @@
     below = (lat > 0).astype(F32)
     above = (lat < lax.axis_size("lat") - 1).astype(F32)
     inside = [[below, below, 1.0], [1.0, above, above]]
+    slots = [[0, 1, 2], [2, 0, 1]]
     profile = filter_ref[...]
     band = band_ref[...].astype(F32)
     source = lax.broadcasted_iota(jnp.int32, (lons, places), 0)
@@ -127,9 +128,10 @@
             for row in range(rows):
                 for tap in range(taps):
                     weight = band[tap, row : row + 1, basis : basis + 1] * inside[row][tap]
-                    table_ref[row, at : at + step, tap * places : (tap + 1) * places] = (
-                        weight * turned
-                    ).astype(BF16)
+                    to = slots[row][tap] * places
+                    table_ref[row, at : at + step, to : to + places] = (weight * turned).astype(
+                        BF16
+                    )
 
 
 def squares_kernel(own_ref, mate_ref, squares_ref, padded):
@@ -157,50 +159,88 @@
         )
 
 
-def conv_kernel(block, width, *refs):
-    odd_mate, odd_own, even_mate, mate, even_own, home = refs[:6]
-    (table_ref, squares_ref), refs = refs[6:8], refs[8:]
-    sources = ((home, mate), (even_own, even_mate), (odd_own, odd_mate))
+def rows_of(message, block, rest):
+    groups = unfold(message.astype(F32), block)
+    last = (groups[2], pltpu.roll(groups[2], SUBLANES - rest, 0))
+    return [jnp.concatenate([groups[row], last[row]], axis=0) for row in range(2)]
+
+
+def both_sides(near, far, side, at):
+    return jnp.where(side == at % 2, near[at // 2].astype(F32), far[at // 2].astype(F32))
+
+
+def mix(over, squares_ref, spread):
+    bases = spread.shape[1] // squares_ref.shape[1]
+    lanes = squares_ref.shape[1]
+    half = spread.shape[0]
+    over = over.astype(BF16)
+    for basis in range(bases):
+        spread[:, basis * lanes : (basis + 1) * lanes] = over[basis * half : (basis + 1) * half]
+    return jnp.dot(spread[...], squares_ref[...], preferred_element_type=F32)
+
+
+def early_kernel(
+    block,
+    width,
+    even_mate,
+    mate,
+    even_own,
+    home,
+    table_ref,
+    squares_ref,
+    mixed_ref,
+    part_ref,
+    field,
+    own_field,
+    spread,
+):
+    columns = home.shape[0]
+    places = table_ref.shape[2] // 3
+    step = places // (2 * columns)
+    rest = width - SUBLANES
+    side = lax.axis_index("lon") % 2
+    odd = lax.axis_index("lat") % 2
+    for at in range(2 * columns):
+        own = rows_of(both_sides(home, mate, side, at), block, rest)
+        near = rows_of(both_sides(even_own, even_mate, side, at), block, rest)
+        first = jnp.where(odd == 1, own[0], own[1])
+        second = jnp.where(odd == 1, own[1], own[0])
+        for slot, read in enumerate(near + [first]):
+            field[slot * places + at * step : slot * places + (at + 1) * step] = read.astype(BF16)
+        own_field[at * step : (at + 1) * step] = second.astype(BF16)
+    part_ref[...] = jnp.dot(
+        table_ref[odd][:, 2 * places :], own_field[...], preferred_element_type=F32
+    )
+    over = jnp.dot(table_ref[1 - odd], field[...], preferred_element_type=F32)
+    mixed_ref[...] = mix(over, squares_ref, spread)
+
+
+def late_kernel(
+    block, width, odd_mate, odd_own, mixed_ref, part_ref, table_ref, squares_ref, *refs
+):
     *out_refs, field, spread, stage = refs
     columns = len(out_refs)
     lanes = squares_ref.shape[1]
-    bases = squares_ref.shape[0] // lanes
-    rows, _, inner = table_ref.shape
-    places = inner // 3
+    places = table_ref.shape[2] // 3
     step = places // (2 * columns)
-    half = places // 2
     rest = width - SUBLANES
     column, side = column_and_side()
-    odd = lax.axis_index("lat") % 2 == 1
+    odd = lax.axis_index("lat") % 2
     for at in range(2 * columns):
-        here = side == at % 2
-        own, even, other = (
-            jnp.where(here, near[at // 2].astype(F32), far[at // 2].astype(F32))
-            for near, far in sources
-        )
-        low = jnp.where(odd, even, other)
-        high = jnp.where(odd, other, even)
-        read = []
-        for message in (low, own, high):
-            groups = unfold(message, block)
-            for row in range(rows):
-                last = pltpu.roll(groups[2], SUBLANES - row * rest, 0) if row else groups[2]
-                read.append(jnp.concatenate([groups[row], last], axis=0).astype(BF16))
-        for row in range(rows):
-            for tap in range(3):
-                first = tap * places + at * step
-                field[row, first : first + step] = read[row * 3 + tap]
-    for row in range(rows):
-        over = jnp.dot(table_ref[row], field[row], preferred_element_type=F32).astype(BF16)
-        for basis in range(bases):
-            spread[row * half : (row + 1) * half, basis * lanes : (basis + 1) * lanes] = over[
-                basis * half : (basis + 1) * half
-            ]
-    mixed = jnp.dot(spread[...], squares_ref[...], preferred_element_type=F32)
+        far = rows_of(both_sides(odd_own, odd_mate, side, at), block, rest)
+        for slot, read in enumerate(far):
+            field[slot * places + at * step : slot * places + (at + 1) * step] = read.astype(BF16)
+    over = part_ref[...] + jnp.dot(
+        table_ref[odd][:, : 2 * places], field[...], preferred_element_type=F32
+    )
+    late = mix(over, squares_ref, spread)
+    early = mixed_ref[...]
+    tops = jnp.where(odd == 1, early, late)
+    bottoms = jnp.where(odd == 1, late, early)
     upper = lax.broadcasted_iota(jnp.int32, (SUBLANES, lanes), 0) < rest
     for target in range(columns):
-        top = mixed[target * step : (target + 1) * step]
-        bottom = mixed[half + target * step : half + (target + 1) * step]
+        top = tops[target * step : (target + 1) * step]
+        bottom = bottoms[target * step : (target + 1) * step]
         last = jnp.where(upper, top[SUBLANES:], pltpu.roll(bottom[SUBLANES:], rest, 0))
         points = jnp.concatenate([top[:SUBLANES], bottom[:SUBLANES], last], axis=0)
         stage[target] = fold(points, block)
@@ -287,11 +327,11 @@
         ]
         return lax.ppermute(block, ("lat", "lon"), pairs)
 
-    odd_mate = swap(lat_odd, 1)
     even_mate = swap(lat_even, 1)
-    odd_own = swap(lat_odd, 0)
     mate = swap(lat_self, 1)
     even_own = swap(lat_even, 0)
+    odd_mate = swap(lat_odd, 1)
+    odd_own = swap(lat_odd, 0)
     return odd_mate, odd_own, even_mate, mate, even_own
 
 
@@ -350,19 +390,34 @@
         10**8,
         *[arrived[apart] for apart in far_first],
     )
-    sources = around(own_side, count)
+    odd_mate, odd_own, even_mate, mate, even_own = around(own_side, count)
+    inner = bases * places // 2
+    spread = pltpu.VMEM((places // 2, bases * lanes), BF16)
+    early = call(
+        functools.partial(early_kernel, block, width),
+        "conv_early",
+        (
+            jax.ShapeDtypeStruct((places // 2, lanes), F32),
+            jax.ShapeDtypeStruct((inner, lanes), F32),
+        ),
+        [pltpu.VMEM((3 * places, lanes), BF16), pltpu.VMEM((places, lanes), BF16), spread],
+        10**9,
+        even_mate,
+        mate,
+        even_own,
+        own_side,
+        table,
+        squares,
+    )
     mixed = call(
-        functools.partial(conv_kernel, block, width),
-        "conv",
+        functools.partial(late_kernel, block, width),
+        "conv_late",
         messages,
-        [
-            pltpu.VMEM((rows, taps * places, lanes), BF16),
-            pltpu.VMEM((rows * places // 2, bases * lanes), BF16),
-            stage,
-        ],
+        [pltpu.VMEM((2 * places, lanes), BF16), spread, stage],
         10**10,
-        *sources,
-        own_side,
+        odd_mate,
+        odd_own,
+        *early,
         table,
         squares,
     )

time: 26.7 us -> 26.5 us (level)
  waiting for transfers between devices: 5.42 us -> 4.76 us
  Pallas kernels: 3.79 us -> 4.31 us
    ppermute x5, waiting for transfers between devices: 1.92 us -> 1.27 us  [swap(): return lax.ppermute(block, ('lat', 'lon'), pairs)]
    pallas_call x6 -> x7, Pallas kernels: 3.79 us -> 4.31 us  [call(): pl.pallas_call(kernel, out_shape=out_shape, in_specs=[VMEM] * len(operand...]
  transfers between devices with their start and end apart: 12 -> 12, of which waited for: 6 -> 6; matrix products, arithmetic and copies ran while one was open for 0% -> 0% of each run, Pallas kernels for 4% -> 7%
where the time goes in v1:
time: 26.5 us; the launch traced here: 26.4 us
  starting transfers between devices  16.4 us (62%)
  waiting for transfers between devices  4.76 us (18%)
  Pallas kernels  4.31 us (16%)
  local copies, waits for them, and re-layouts  0.77 us (3%)
    ppermute x6, starting transfers between devices, over_columns(): arrived[apart] = lax.ppermute(messages[apart], 'lon', pairs)  10.2 us
    ppermute x5, starting transfers between devices, swap(): return lax.ppermute(block, ('lat', 'lon'), pairs)  4.59 us
    pallas_call x7, Pallas kernels, call(): pl.pallas_call(kernel, out_shape=out_shape, in_specs=[VMEM] * len(operand...  4.31 us
    ppermute x6, waiting for transfers between devices, over_columns(): arrived[apart] = lax.ppermute(messages[apart], 'lon', pairs)  3.49 us
    ppermute x1, starting transfers between devices, over_sides(): return lax.ppermute(block, 'lon', [(i, i ^ 1) for i in range(count)])  1.63 us
    ppermute x5, waiting for transfers between devices, swap(): return lax.ppermute(block, ('lat', 'lon'), pairs)  1.27 us
    unnamed x14, local copies, waits for them, and re-layouts  0.77 us
  transfers between devices with their start and end apart: 12, of which 6 were waited for; matrix products, arithmetic and copies ran while one was open for 0% of the time, Pallas kernels for 7%

profile of v1, /device:TPU:0, one launch (start us, length us, event | category | flops | bytes accessed | tf_op | source)
XLA Modules:
  0.0 26.4 jit_solution(1529989219534494116)
XLA Ops:
  0.0 0.0 copy-start.3
  0.0 0.8 %copy-done.3 = bf16[2,12,640]{2,0,1:T(2,128)(2,1)S(1)} copy-done((bf16[2,12,640]{2,0,1:T(2,128)(2,1)S(1)}, bf16[2,12,640]{2,0,1:T(2,128)(2,1)}, u32[]{:S(2)}) %copy-start.3) | copy-done | bytes 30744
  0.8 0.0 copy-start.2
  0.8 0.0 copy-start.5
  0.8 0.0 copy-start.6
  0.8 0.2 pack.1
  0.9 5.1 %collective-permute-start = (bf16[32,128]{1,0:T(8,128)(2,1)S(1)}, bf16[32,128]{1,0:T(8,128)(2,1)S(1)}, u32[]{:S(2)}, u32[]{:S(2)}) collective-permute-start(bf16[32,128]{1,0:T(8,128)(2,1)S(1)} %get-tuple-element.15), channel_id=1, source_target_pairs={{0,6},{1,7},{2,4},{3,5},{4,2},{5,3},{6,0},{7,1},{8,14},{9,15},{10,... | collective-permute-start | bytes 24584 | tf_op jit(solution)/shard_map/ppermute | solution.py:307
  6.1 0.0 collective-permute-start.1
  6.1 0.6 %collective-permute-start.2 = (bf16[32,128]{1,0:T(8,128)(2,1)S(1)}, bf16[32,128]{1,0:T(8,128)(2,1)S(1)}, u32[]{:S(2)}, u32[]{:S(2)}) collective-permute-start(bf16[32,128]{1,0:T(8,128)(2,1)S(1)} %get-tuple-element.17), channel_id=1, source_target_pairs={{0,2},{1,3},{2,0},{3,1},{4,6},{5,7},{6,4},{7,5},{8,10},{9,11},{10,... | collective-permute-start | bytes 24584 | tf_op jit(solution)/shard_map/ppermute | solution.py:307
  6.7 0.0 copy-done.2
  6.7 1.6 %collective-permute-start.8 = (bf16[9,20,80]{2,1,0:T(8,128)(2,1)S(1)}, bf16[9,20,80]{2,1,0:T(8,128)(2,1)S(1)}, u32[]{:S(2)}, u32[]{:S(2)}) collective-permute-start(bf16[9,20,80]{2,1,0:T(8,128)(2,1)S(1)} %bitcast.4), channel_id=1, source_target_pairs={{0,1},{1,0},{2,3},{3,2},{4,5},{5,4},{6,7},{7,6},{8,9},{9,8},{10,11... | collective-permute-start | bytes 86408 | tf_op jit(solution)/shard_map/ppermute | solution.py:312
  8.3 0.0 copy-done.5
  8.3 0.0 copy-done.6
  8.3 0.4 %tables.1.table_ref = bf16[2,576,384]{2,1,0:T(8,128)(2,1)S(1)} custom-call(bf16[9,96]{1,0:T(8,128)(2,1)S(1)} %copy-done.5, bf16[3,2,9]{2,1,0:T(2,128)(2,1)S(1)} %bitcast.8), custom_call_target="tpu_custom_call" | custom-call | flops 1000000000 | bytes 1000000 | tf_op jit(solution)/shard_map/tables/pallas_call | solution.py:291
  8.7 0.0 collective-permute-done.refs_0_
  8.8 1.8 %collective-permute-done.1.refs_1_ = bf16[32,128]{1,0:T(8,128)(2,1)S(1)} collective-permute-done((bf16[32,128]{1,0:T(8,128)(2,1)S(1)}, bf16[32,128]{1,0:T(8,128)(2,1)S(1)}, u32[]{:S(2)}, u32[]{:S(2)}) %collective-permute-start.1) | collective-permute-done | bytes 8224 | tf_op jit(solution)/shard_map/ppermute | solution.py:307
  10.6 0.0 collective-permute-done.2.refs_2_
  10.6 0.1 collective-permute-start.5
  10.7 1.6 %collective-permute-start.6 = (bf16[4,32,128]{2,1,0:T(8,128)(2,1)S(1)}, bf16[4,32,128]{2,1,0:T(8,128)(2,1)S(1)}, u32[]{:S(2)}, u32[]{:S(2)}) collective-permute-start(bf16[4,32,128]{2,1,0:T(8,128)(2,1)S(1)} %join_columns.1.home), channel_id=1, source_target_pairs={{0,1},{1,0},{2,3},{3,2},{4,5},{5,4},{6,7},{7,6},{8,9},{9,8},{10,11... | collective-permute-start | bytes 98312 | tf_op jit(solution)/shard_map/ppermute | solution.py:328
  12.2 0.3 %collective-permute-start.7 = (bf16[4,32,128]{2,1,0:T(8,128)(2,1)S(1)}, bf16[4,32,128]{2,1,0:T(8,128)(2,1)S(1)}, u32[]{:S(2)}, u32[]{:S(2)}) collective-permute-start(bf16[4,32,128]{2,1,0:T(8,128)(2,1)S(1)} %join_columns.1.home), channel_id=1, source_target_pairs={{0,8},{1,9},{2,10},{3,11},{4,12},{5,13},{6,14},{7,15},{8,0},{9,1},... | collective-permute-start | bytes 98312 | tf_op jit(solution)/shard_map/ppermute | solution.py:328
  12.5 2.1 %collective-permute-start.3 = (bf16[4,32,128]{2,1,0:T(8,128)(2,1)S(1)}, bf16[4,32,128]{2,1,0:T(8,128)(2,1)S(1)}, u32[]{:S(2)}, u32[]{:S(2)}) collective-permute-start(bf16[4,32,128]{2,1,0:T(8,128)(2,1)S(1)} %join_columns.1.home), channel_id=1, source_target_pairs={{0,25},{1,24},{2,27},{3,26},{4,29},{5,28},{6,31},{7,30},{8,17},{9,... | collective-permute-start | bytes 98312 | tf_op jit(solution)/shard_map/ppermute | solution.py:328
  14.6 0.0 collective-permute-done.8.mate_ref
  14.6 0.6 %collective-permute-start.4 = (bf16[4,32,128]{2,1,0:T(8,128)(2,1)S(1)}, bf16[4,32,128]{2,1,0:T(8,128)(2,1)S(1)}, u32[]{:S(2)}, u32[]{:S(2)}) collective-permute-start(bf16[4,32,128]{2,1,0:T(8,128)(2,1)S(1)} %join_columns.1.home), channel_id=1, source_target_pairs={{0,24},{1,25},{2,26},{3,27},{4,28},{5,29},{6,30},{7,31},{8,16},{9,... | collective-permute-start | bytes 98312 | tf_op jit(solution)/shard_map/ppermute | solution.py:328
  15.2 0.5 %squares.1.squares_ref = bf16[2304,256]{1,0:T(8,128)(2,1)S(1)} custom-call(bf16[9,20,80]{2,1,0:T(8,128)(2,1)S(1)} %bitcast.5, bf16[9,20,80]{2,1,0:T(8,128)(2,1)S(1)} %collective-permute-done.8.mate_ref), custom_call_target="tpu_custom_call" | custom-call | flops 1000000000 | bytes 1000000 | tf_op jit(solution)/shard_map/squares/pallas_call | solution.py:291
  15.8 0.0 collective-permute-done.5.even_mate
  15.8 0.0 collective-permute-done.6.mate
  15.8 0.0 collective-permute-done.7.even_own
  15.8 0.9 %conv_early.1 = (f32[64,256]{1,0:T(8,128)S(1)}, f32[576,256]{1,0:T(8,128)S(1)}) custom-call(bf16[4,32,128]{2,1,0:T(8,128)(2,1)S(1)} %collective-permute-done.5.even_mate, bf16[4,32,128]{2,1,0:T(8,128)(2,1)S(1)} %collective-permute-done.6.mate, bf16[4,32,128]{2,1,0:T(8,128)(2,1)S(1)} %collective-permute-done.7.even_own, ...), custom_call_target="tpu_custom_call" | custom-call | flops 1000000000 | bytes 1000000 | tf_op jit(solution)/shard_map/conv_early/pallas_call | solution.py:291
  16.7 0.1 collective-permute-done.3.odd_mate
  16.8 1.2 %collective-permute-done.4.odd_own = bf16[4,32,128]{2,1,0:T(8,128)(2,1)S(1)} collective-permute-done((bf16[4,32,128]{2,1,0:T(8,128)(2,1)S(1)}, bf16[4,32,128]{2,1,0:T(8,128)(2,1)S(1)}, u32[]{:S(2)}, u32[]{:S(2)}) %collective-permute-start.4) | collective-permute-done | bytes 32800 | tf_op jit(solution)/shard_map/ppermute | solution.py:328
  17.9 0.0 copy-start
  17.9 0.0 copy-start.1
  17.9 0.0 copy-start.4
  17.9 0.7 %conv_late.1 = (bf16[32,128]{1,0:T(8,128)(2,1)S(1)}, bf16[32,128]{1,0:T(8,128)(2,1)S(1)}, bf16[32,128]{1,0:T(8,128)(2,1)S(1)}, bf16[32,128]{1,0:T(8,128)(2,1)S(1)}) custom-call(bf16[4,32,128]{2,1,0:T(8,128)(2,1)S(1)} %collective-permute-done.3.odd_mate, bf16[4,32,128]{2,1,0:T(8,128)(2,1)S(1)} %collective-permute-done.4.odd_own, ...), custom_call_target="tpu_custom_call" | custom-call | flops 10000000000 | bytes 1000000 | tf_op jit(solution)/shard_map/conv_late/pallas_call | solution.py:291
  18.7 1.5 %collective-permute-start.10 = (bf16[32,128]{1,0:T(8,128)(2,1)S(1)}, bf16[32,128]{1,0:T(8,128)(2,1)S(1)}, u32[]{:S(2)}, u32[]{:S(2)}) collective-permute-start(bf16[32,128]{1,0:T(8,128)(2,1)S(1)} %get-tuple-element.22), channel_id=1, source_target_pairs={{0,6},{1,7},{2,4},{3,5},{4,2},{5,3},{6,0},{7,1},{8,14},{9,15},{10,... | collective-permute-start | bytes 24584 | tf_op jit(solution)/shard_map/ppermute | solution.py:307
  20.1 0.6 %collective-permute-start.11 = (bf16[32,128]{1,0:T(8,128)(2,1)S(1)}, bf16[32,128]{1,0:T(8,128)(2,1)S(1)}, u32[]{:S(2)}, u32[]{:S(2)}) collective-permute-start(bf16[32,128]{1,0:T(8,128)(2,1)S(1)} %get-tuple-element.23), channel_id=1, source_target_pairs={{0,4},{1,5},{2,6},{3,7},{4,0},{5,1},{6,2},{7,3},{8,12},{9,13},{10,... | collective-permute-start | bytes 24584 | tf_op jit(solution)/shard_map/ppermute | solution.py:307
  20.7 2.4 %collective-permute-start.9 = (bf16[32,128]{1,0:T(8,128)(2,1)S(1)}, bf16[32,128]{1,0:T(8,128)(2,1)S(1)}, u32[]{:S(2)}, u32[]{:S(2)}) collective-permute-start(bf16[32,128]{1,0:T(8,128)(2,1)S(1)} %get-tuple-element.21), channel_id=1, source_target_pairs={{0,2},{1,3},{2,0},{3,1},{4,6},{5,7},{6,4},{7,5},{8,10},{9,11},{10,... | collective-permute-start | bytes 24584 | tf_op jit(solution)/shard_map/ppermute | solution.py:307
  23.1 1.1 %collective-permute-done.10.refs_1_ = bf16[32,128]{1,0:T(8,128)(2,1)S(1)} collective-permute-done((bf16[32,128]{1,0:T(8,128)(2,1)S(1)}, bf16[32,128]{1,0:T(8,128)(2,1)S(1)}, u32[]{:S(2)}, u32[]{:S(2)}) %collective-permute-start.10) | collective-permute-done | bytes 8224 | tf_op jit(solution)/shard_map/ppermute | solution.py:307
  24.2 0.5 %collective-permute-done.11.refs_2_ = bf16[32,128]{1,0:T(8,128)(2,1)S(1)} collective-permute-done((bf16[32,128]{1,0:T(8,128)(2,1)S(1)}, bf16[32,128]{1,0:T(8,128)(2,1)S(1)}, u32[]{:S(2)}, u32[]{:S(2)}) %collective-permute-start.11) | collective-permute-done | bytes 8224 | tf_op jit(solution)/shard_map/ppermute | solution.py:307
  24.7 0.1 collective-permute-done.9.refs_0_
  24.7 0.0 copy-done
  24.8 0.0 copy-done.1
  24.8 0.0 copy-done.4
  24.8 1.6 %tail.1 = bf16[12,2,640]{2,1,0:T(2,128)(2,1)} custom-call(bf16[32,128]{1,0:T(8,128)(2,1)S(1)} %collective-permute-done.9.refs_0_, bf16[32,128]{1,0:T(8,128)(2,1)S(1)} %collective-permute-done.10.refs_1_, bf16[32,128]{1,0:T(8,128)(2,1)S(1)} %collective-permute-done.11.refs_2_, bf16[32,128]{1,0:T(8,128)(2,1)S(1)} %get-tuple-element.24.refs_3_, ...), custom_call_target="tpu_custom_call" | custom-call | flops 1000000000 | bytes 1000000 | tf_op jit(solution)/shard_map/tail/pallas_call | solution.py:291
  (1 shorter events, 0.0 us)
Async XLA Ops:
  0.0 0.8 %copy-start.3 = (bf16[2,12,640]{2,0,1:T(2,128)(2,1)S(1)}, bf16[2,12,640]{2,0,1:T(2,128)(2,1)}, u32[]{:S(2)}) copy-start(bf16[2,12,640]{2,0,1:T(2,128)(2,1)} %param.7) | copy-start | bytes 92164
  0.8 5.9 %copy-start.2 = (bf16[9,80,20]{1,2,0:T(8,128)(2,1)S(1)}, bf16[9,80,20]{1,2,0:T(8,128)(2,1)}, u32[]{:S(2)}) copy-start(bf16[9,80,20]{1,2,0:T(8,128)(2,1)} %param.9) | copy-start | bytes 86404
  0.8 7.6 %copy-start.5 = (bf16[9,96]{1,0:T(8,128)(2,1)S(1)}, bf16[9,96]{1,0:T(8,128)(2,1)}, u32[]{:S(2)}) copy-start(bf16[9,96]{1,0:T(8,128)(2,1)} %filter_ref.1) | copy-start | bytes 5188
  0.8 7.6 %copy-start.6 = (bf16[9,2,3]{0,1,2:T(2,128)(2,1)S(1)}, bf16[9,2,3]{0,1,2:T(2,128)(2,1)}, u32[]{:S(2)}) copy-start(bf16[9,2,3]{0,1,2:T(2,128)(2,1)} %param.10) | copy-start | bytes 328
  0.9 7.8 %collective-permute-start = (bf16[32,128]{1,0:T(8,128)(2,1)S(1)}, bf16[32,128]{1,0:T(8,128)(2,1)S(1)}, u32[]{:S(2)}, u32[]{:S(2)}) collective-permute-start(bf16[32,128]{1,0:T(8,128)(2,1)S(1)} %get-tuple-element.15), channel_id=1, source_target_pairs={{0,6},{1,7},{2,4},{3,5},{4,2},{5,3},{6,0},{7,1},{8,14},{9,15},{10,... | collective-permute-start | bytes 24584 | tf_op jit(solution)/shard_map/ppermute | solution.py:307
  6.1 4.5 %collective-permute-start.1 = (bf16[32,128]{1,0:T(8,128)(2,1)S(1)}, bf16[32,128]{1,0:T(8,128)(2,1)S(1)}, u32[]{:S(2)}, u32[]{:S(2)}) collective-permute-start(bf16[32,128]{1,0:T(8,128)(2,1)S(1)} %get-tuple-element.16), channel_id=1, source_target_pairs={{0,4},{1,5},{2,6},{3,7},{4,0},{5,1},{6,2},{7,3},{8,12},{9,13},{10,... | collective-permute-start | bytes 24584 | tf_op jit(solution)/shard_map/ppermute | solution.py:307
  6.1 4.5 %collective-permute-start.2 = (bf16[32,128]{1,0:T(8,128)(2,1)S(1)}, bf16[32,128]{1,0:T(8,128)(2,1)S(1)}, u32[]{:S(2)}, u32[]{:S(2)}) collective-permute-start(bf16[32,128]{1,0:T(8,128)(2,1)S(1)} %get-tuple-element.17), channel_id=1, source_target_pairs={{0,2},{1,3},{2,0},{3,1},{4,6},{5,7},{6,4},{7,5},{8,10},{9,11},{10,... | collective-permute-start | bytes 24584 | tf_op jit(solution)/shard_map/ppermute | solution.py:307
  6.7 7.9 %collective-permute-start.8 = (bf16[9,20,80]{2,1,0:T(8,128)(2,1)S(1)}, bf16[9,20,80]{2,1,0:T(8,128)(2,1)S(1)}, u32[]{:S(2)}, u32[]{:S(2)}) collective-permute-start(bf16[9,20,80]{2,1,0:T(8,128)(2,1)S(1)} %bitcast.4), channel_id=1, source_target_pairs={{0,1},{1,0},{2,3},{3,2},{4,5},{5,4},{6,7},{7,6},{8,9},{9,8},{10,11... | collective-permute-start | bytes 86408 | tf_op jit(solution)/shard_map/ppermute | solution.py:312
  10.6 5.2 %collective-permute-start.5 = (bf16[4,32,128]{2,1,0:T(8,128)(2,1)S(1)}, bf16[4,32,128]{2,1,0:T(8,128)(2,1)S(1)}, u32[]{:S(2)}, u32[]{:S(2)}) collective-permute-start(bf16[4,32,128]{2,1,0:T(8,128)(2,1)S(1)} %join_columns.1.home), channel_id=1, source_target_pairs={{0,9},{1,8},{2,11},{3,10},{4,13},{5,12},{6,15},{7,14},{8,1},{9,0},... | collective-permute-start | bytes 98312 | tf_op jit(solution)/shard_map/ppermute | solution.py:328
  10.7 5.1 %collective-permute-start.6 = (bf16[4,32,128]{2,1,0:T(8,128)(2,1)S(1)}, bf16[4,32,128]{2,1,0:T(8,128)(2,1)S(1)}, u32[]{:S(2)}, u32[]{:S(2)}) collective-permute-start(bf16[4,32,128]{2,1,0:T(8,128)(2,1)S(1)} %join_columns.1.home), channel_id=1, source_target_pairs={{0,1},{1,0},{2,3},{3,2},{4,5},{5,4},{6,7},{7,6},{8,9},{9,8},{10,11... | collective-permute-start | bytes 98312 | tf_op jit(solution)/shard_map/ppermute | solution.py:328
  12.2 3.5 %collective-permute-start.7 = (bf16[4,32,128]{2,1,0:T(8,128)(2,1)S(1)}, bf16[4,32,128]{2,1,0:T(8,128)(2,1)S(1)}, u32[]{:S(2)}, u32[]{:S(2)}) collective-permute-start(bf16[4,32,128]{2,1,0:T(8,128)(2,1)S(1)} %join_columns.1.home), channel_id=1, source_target_pairs={{0,8},{1,9},{2,10},{3,11},{4,12},{5,13},{6,14},{7,15},{8,0},{9,1},... | collective-permute-start | bytes 98312 | tf_op jit(solution)/shard_map/ppermute | solution.py:328
  12.5 4.2 %collective-permute-start.3 = (bf16[4,32,128]{2,1,0:T(8,128)(2,1)S(1)}, bf16[4,32,128]{2,1,0:T(8,128)(2,1)S(1)}, u32[]{:S(2)}, u32[]{:S(2)}) collective-permute-start(bf16[4,32,128]{2,1,0:T(8,128)(2,1)S(1)} %join_columns.1.home), channel_id=1, source_target_pairs={{0,25},{1,24},{2,27},{3,26},{4,29},{5,28},{6,31},{7,30},{8,17},{9,... | collective-permute-start | bytes 98312 | tf_op jit(solution)/shard_map/ppermute | solution.py:328
  14.6 3.3 %collective-permute-start.4 = (bf16[4,32,128]{2,1,0:T(8,128)(2,1)S(1)}, bf16[4,32,128]{2,1,0:T(8,128)(2,1)S(1)}, u32[]{:S(2)}, u32[]{:S(2)}) collective-permute-start(bf16[4,32,128]{2,1,0:T(8,128)(2,1)S(1)} %join_columns.1.home), channel_id=1, source_target_pairs={{0,24},{1,25},{2,26},{3,27},{4,28},{5,29},{6,30},{7,31},{8,16},{9,... | collective-permute-start | bytes 98312 | tf_op jit(solution)/shard_map/ppermute | solution.py:328
  17.9 6.8 %copy-start = (bf16[640,1280]{1,0:T(8,128)(2,1)S(1)}, bf16[640,1280]{1,0:T(8,128)(2,1)}, u32[]{:S(2)}) copy-start(bf16[640,1280]{1,0:T(8,128)(2,1)} %refs_5_.1) | copy-start | bytes 4915204
  17.9 6.8 %copy-start.1 = (bf16[1280,640]{1,0:T(8,128)(2,1)S(1)}, bf16[1280,640]{1,0:T(8,128)(2,1)}, u32[]{:S(2)}) copy-start(bf16[1280,640]{1,0:T(8,128)(2,1)} %refs_6_.1) | copy-start | bytes 4915204
  17.9 6.8 %copy-start.4 = (bf16[2,12,640]{2,0,1:T(2,128)(2,1)S(1)}, bf16[2,12,640]{2,0,1:T(2,128)(2,1)}, u32[]{:S(2)}) copy-start(bf16[2,12,640]{2,0,1:T(2,128)(2,1)} %param.7) | copy-start | bytes 92164
  18.7 5.5 %collective-permute-start.10 = (bf16[32,128]{1,0:T(8,128)(2,1)S(1)}, bf16[32,128]{1,0:T(8,128)(2,1)S(1)}, u32[]{:S(2)}, u32[]{:S(2)}) collective-permute-start(bf16[32,128]{1,0:T(8,128)(2,1)S(1)} %get-tuple-element.22), channel_id=1, source_target_pairs={{0,6},{1,7},{2,4},{3,5},{4,2},{5,3},{6,0},{7,1},{8,14},{9,15},{10,... | collective-permute-start | bytes 24584 | tf_op jit(solution)/shard_map/ppermute | solution.py:307
  20.1 4.6 %collective-permute-start.11 = (bf16[32,128]{1,0:T(8,128)(2,1)S(1)}, bf16[32,128]{1,0:T(8,128)(2,1)S(1)}, u32[]{:S(2)}, u32[]{:S(2)}) collective-permute-start(bf16[32,128]{1,0:T(8,128)(2,1)S(1)} %get-tuple-element.23), channel_id=1, source_target_pairs={{0,4},{1,5},{2,6},{3,7},{4,0},{5,1},{6,2},{7,3},{8,12},{9,13},{10,... | collective-permute-start | bytes 24584 | tf_op jit(solution)/shard_map/ppermute | solution.py:307
  20.7 4.0 %collective-permute-start.9 = (bf16[32,128]{1,0:T(8,128)(2,1)S(1)}, bf16[32,128]{1,0:T(8,128)(2,1)S(1)}, u32[]{:S(2)}, u32[]{:S(2)}) collective-permute-start(bf16[32,128]{1,0:T(8,128)(2,1)S(1)} %get-tuple-element.21), channel_id=1, source_target_pairs={{0,2},{1,3},{2,0},{3,1},{4,6},{5,7},{6,4},{7,5},{8,10},{9,11},{10,... | collective-permute-start | bytes 24584 | tf_op jit(solution)/shard_map/ppermute | solution.py:307

commit v2 on v0

--- a/solution.py
+++ b/solution.py
@@ -74,26 +74,17 @@
         points[at : at + rest] = latent_ref[SUBLANES:, row, :].astype(F32)
 
 
-def pack_kernel(latent_ref, *refs):
-    *out_refs, points, stage = refs
-    columns = len(out_refs)
+def pack_kernel(latent_ref, out_ref, points):
+    columns = out_ref.shape[0] // 2
     chans = latent_ref.shape[2]
     block = chans // columns
-    column, _ = column_and_side()
     group_points(latent_ref, points)
     own = points[...]
     for target in range(columns):
         turned = pltpu.roll(own, chans - target * block, 1) if target else own
-        stage[target] = fold(turned[:, : lanes_of(block)], block)
-    for apart in range(columns):
-        out_refs[apart][...] = stage[column ^ apart]
-
-
-def column_kernel(order, *refs):
-    *in_refs, out_ref = refs
-    column, _ = column_and_side()
-    for apart, ref in zip(order, in_refs):
-        out_ref[column ^ apart] = ref[...]
+        message = fold(turned[:, : lanes_of(block)], block)
+        out_ref[2 * target] = message
+        out_ref[2 * target + 1] = message
 
 
 def tables_kernel(width, filter_ref, band_ref, table_ref, first):
@@ -158,9 +149,7 @@
 
 
 def conv_kernel(block, width, *refs):
-    odd_mate, odd_own, even_mate, mate, even_own, home = refs[:6]
-    (table_ref, squares_ref), refs = refs[6:8], refs[8:]
-    sources = ((home, mate), (even_own, even_mate), (odd_own, odd_mate))
+    odd_refs, even_refs, home, table_ref, squares_ref, *refs = refs
     *out_refs, field, spread, stage = refs
     columns = len(out_refs)
     lanes = squares_ref.shape[1]
@@ -170,14 +159,10 @@
     step = places // (2 * columns)
     half = places // 2
     rest = width - SUBLANES
-    column, side = column_and_side()
+    column, _ = column_and_side()
     odd = lax.axis_index("lat") % 2 == 1
     for at in range(2 * columns):
-        here = side == at % 2
-        own, even, other = (
-            jnp.where(here, near[at // 2].astype(F32), far[at // 2].astype(F32))
-            for near, far in sources
-        )
+        own, even, other = (ref[at].astype(F32) for ref in (home, even_refs, odd_refs))
         low = jnp.where(odd, even, other)
         high = jnp.where(odd, other, even)
         read = []
@@ -272,27 +257,11 @@
     return lax.ppermute(block, "lon", [(i, i ^ 1) for i in range(count)])
 
 
-def around(block, count):
+def over_rows(block):
     rows = lax.axis_size("lat")
-    lat_even = [i ^ 1 for i in range(rows)]
-    lat_odd = [((i - 1) ^ 1) + 1 if i else rows - 1 for i in range(rows)]
-    lat_odd[rows - 1] = 0
-    lat_self = list(range(rows))
-
-    def swap(lat_of, other_side):
-        pairs = [
-            (lat * count + lon, lat_of[lat] * count + (lon ^ other_side))
-            for lat in range(rows)
-            for lon in range(count)
-        ]
-        return lax.ppermute(block, ("lat", "lon"), pairs)
-
-    odd_mate = swap(lat_odd, 1)
-    even_mate = swap(lat_even, 1)
-    odd_own = swap(lat_odd, 0)
-    mate = swap(lat_self, 1)
-    even_own = swap(lat_even, 0)
-    return odd_mate, odd_own, even_mate, mate, even_own
+    odd = [(i, (i + 1 if i % 2 else i - 1) % rows) for i in range(rows)]
+    even = [(i, i ^ 1) for i in range(rows)]
+    return lax.ppermute(block, "lat", odd), lax.ppermute(block, "lat", even)
 
 
 def local(latent, lon_filter, mix_weight, band_weight, offsets, w_up, w_down):
@@ -308,11 +277,11 @@
     lanes = lanes_of(block)
     height = message_rows(block)
     assert rows == 2 and taps == 3 and columns & (columns - 1) == 0
+    assert lax.axis_size("lat") % 2 == 0
     assert SUBLANES < width and rows * (width - SUBLANES) <= SUBLANES
     assert 3 * (block % LANES) <= LANES
 
     far_first = tuple(reversed(range(columns)))
-    near_then_far = (1,) + tuple(reversed(range(2, columns))) + (0,)
     message = jax.ShapeDtypeStruct((height, LANES), BF16)
     messages = (message,) * columns
     stage = pltpu.VMEM((columns, height, LANES), BF16)
@@ -320,15 +289,16 @@
     lon_first = jnp.transpose(latent, (1, 0, 2))
     mix_own = jnp.transpose(mix_weight, (0, 2, 1))
 
-    packed = call(pack_kernel, "pack", messages, [points, stage], 10**9, lon_first)
-    arrived = over_columns(packed, count)
+    circle = jax.ShapeDtypeStruct((count, height, LANES), BF16)
+    packed = call(pack_kernel, "pack", circle, [points], 10**9, lon_first)
+    home = lax.all_to_all(packed, "lon", split_axis=0, concat_axis=0, tiled=True)
     mix_mate = over_sides(mix_own, count)
     table = call(
         functools.partial(tables_kernel, width),
         "tables",
         jax.ShapeDtypeStruct((rows, bases * places // 2, taps * places), BF16),
         [pltpu.VMEM((bases, step, places), F32)],
-        10**9,
+        10**6,
         lon_filter,
         jnp.transpose(band_weight, (2, 1, 0)),
     )
@@ -337,20 +307,11 @@
         "squares",
         jax.ShapeDtypeStruct((bases * lanes, lanes), BF16),
         [pltpu.VMEM((2, bases, up_to(group, 2 * SUBLANES), lanes), F32)],
-        10**9,
+        2 * 10**10,
         mix_own,
         mix_mate,
     )
-    gathered = jax.ShapeDtypeStruct((columns, height, LANES), BF16)
-    own_side = call(
-        functools.partial(column_kernel, far_first),
-        "join_columns",
-        gathered,
-        [],
-        10**8,
-        *[arrived[apart] for apart in far_first],
-    )
-    sources = around(own_side, count)
+    odd, even = over_rows(home)
     mixed = call(
         functools.partial(conv_kernel, block, width),
         "conv",
@@ -361,19 +322,20 @@
             stage,
         ],
         10**10,
-        *sources,
-        own_side,
+        odd,
+        even,
+        home,
         table,
         squares,
     )
     back = over_columns(mixed, count)
     result = call(
-        functools.partial(tail_kernel, near_then_far),
+        functools.partial(tail_kernel, far_first),
         "tail",
         jax.ShapeDtypeStruct(lon_first.shape, BF16),
         [points, stage],
         10**9,
-        *[back[apart] for apart in near_then_far],
+        *[back[apart] for apart in far_first],
         lon_first,
         w_up,
         w_down,

time: 26.7 us -> 29 us (1.086)
  waiting for transfers between devices: 5.42 us -> 8.18 us
  starting transfers between devices: 16.4 us -> 15.4 us
  Pallas kernels: 3.79 us -> 4.4 us
    all_to_all x0 -> x1, starting transfers between devices: none -> 7.25 us  [local(): lax.all_to_all(packed, 'lon', split_axis=0, concat_axis=0, tiled=True)]
    ppermute x6 -> x3, starting transfers between devices: 10.2 us -> 4.45 us  [over_columns(): arrived[apart] = lax.ppermute(messages[apart], 'lon', pairs)]
    all_to_all x0 -> x1, waiting for transfers between devices: none -> 4.47 us  [local(): lax.all_to_all(packed, 'lon', split_axis=0, concat_axis=0, tiled=True)]
    ppermute x5 -> x2, starting transfers between devices: 4.6 us -> 1.63 us  [over_rows(): return (lax.ppermute(block, 'lat', odd), lax.ppermute(block, 'lat', even))]
    ppermute x6 -> x3, waiting for transfers between devices: 3.49 us -> 1.63 us  [over_columns(): arrived[apart] = lax.ppermute(messages[apart], 'lon', pairs)]
    pallas_call x6 -> x5, Pallas kernels: 3.79 us -> 4.4 us  [call(): pl.pallas_call(kernel, out_shape=out_shape, in_specs=[VMEM] * len(operand...]
    ppermute x1, starting transfers between devices: 1.63 us -> 2.02 us  [over_sides(): return lax.ppermute(block, 'lon', [(i, i ^ 1) for i in range(count)])]
    ppermute x5 -> x2, waiting for transfers between devices: 1.92 us -> 2.08 us  [over_rows(): return (lax.ppermute(block, 'lat', odd), lax.ppermute(block, 'lat', even))]
  transfers between devices with their start and end apart: 12 -> 7, of which waited for: 6 -> 4; matrix products, arithmetic and copies ran while one was open for 0% -> 0% of each run, Pallas kernels for 4% -> 3%
where the time goes in v2:
time: 29 us; the launch traced here: 28.8 us
  starting transfers between devices  15.4 us (53%)
  waiting for transfers between devices  8.18 us (28%)
  Pallas kernels  4.4 us (15%)
  local copies, waits for them, and re-layouts  0.78 us (3%)
    all_to_all x1, starting transfers between devices, local(): lax.all_to_all(packed, 'lon', split_axis=0, concat_axis=0, tiled=True)  7.25 us
    all_to_all x1, waiting for transfers between devices, local(): lax.all_to_all(packed, 'lon', split_axis=0, concat_axis=0, tiled=True)  4.47 us
    ppermute x3, starting transfers between devices, over_columns(): arrived[apart] = lax.ppermute(messages[apart], 'lon', pairs)  4.45 us
    pallas_call x5, Pallas kernels, call(): pl.pallas_call(kernel, out_shape=out_shape, in_specs=[VMEM] * len(operand...  4.4 us
    ppermute x2, waiting for transfers between devices, over_rows(): return (lax.ppermute(block, 'lat', odd), lax.ppermute(block, 'lat', even))  2.08 us
    ppermute x1, starting transfers between devices, over_sides(): return lax.ppermute(block, 'lon', [(i, i ^ 1) for i in range(count)])  2.02 us
    ppermute x2, starting transfers between devices, over_rows(): return (lax.ppermute(block, 'lat', odd), lax.ppermute(block, 'lat', even))  1.63 us
    ppermute x3, waiting for transfers between devices, over_columns(): arrived[apart] = lax.ppermute(messages[apart], 'lon', pairs)  1.63 us
  transfers between devices with their start and end apart: 7, of which 4 were waited for; matrix products, arithmetic and copies ran while one was open for 0% of the time, Pallas kernels for 3%

profile of v2, /device:TPU:0, one launch (start us, length us, event | category | flops | bytes accessed | tf_op | source)
XLA Modules:
  0.0 28.8 jit_solution(11673361993354142216)
XLA Ops:
  0.0 0.0 copy-start.5
  0.0 0.8 %copy-done.5 = bf16[2,12,640]{2,0,1:T(2,128)(2,1)S(1)} copy-done((bf16[2,12,640]{2,0,1:T(2,128)(2,1)S(1)}, bf16[2,12,640]{2,0,1:T(2,128)(2,1)}, u32[]{:S(2)}) %copy-start.5) | copy-done | bytes 30744
  0.8 0.0 copy-start.4
  0.8 0.0 copy-start
  0.8 0.0 copy-start.1
  0.8 0.8 %pack.1 = bf16[8,32,128]{2,1,0:T(8,128)(2,1)} custom-call(bf16[12,2,640]{2,1,0:T(2,128)(2,1)S(1)} %bitcast.7), custom_call_target="tpu_custom_call" | custom-call | flops 1000000000 | bytes 1000000 | tf_op jit(solution)/shard_map/pack/pallas_call | solution.py:236
  1.6 7.3 %all-to-all-start = ((bf16[8,32,128]{2,1,0:T(8,128)(2,1)}), bf16[8,32,128]{2,1,0:T(8,128)(2,1)S(1)}, u32[]{:S(2)}, u32[]{:S(2)}) async-start(bf16[8,32,128]{2,1,0:T(8,128)(2,1)} %pack.1), calls=%async_computation | async-start | bytes 131072 | tf_op jit(solution)/shard_map/all_to_all | solution.py:294
  8.8 0.0 copy-done.4
  8.8 2.0 %collective-permute-start.2 = (bf16[9,20,80]{2,1,0:T(8,128)(2,1)S(1)}, bf16[9,20,80]{2,1,0:T(8,128)(2,1)S(1)}, u32[]{:S(2)}, u32[]{:S(2)}) collective-permute-start(bf16[9,20,80]{2,1,0:T(8,128)(2,1)S(1)} %bitcast.5), channel_id=1, source_target_pairs={{0,1},{1,0},{2,3},{3,2},{4,5},{5,4},{6,7},{7,6},{8,9},{9,8},{10,11... | collective-permute-start | bytes 86408 | tf_op jit(solution)/shard_map/ppermute | solution.py:257
  10.8 0.0 copy-done
  10.8 0.0 copy-done.1
  10.8 0.4 %tables.1.refs_3_ = bf16[2,576,384]{2,1,0:T(8,128)(2,1)S(1)} custom-call(bf16[9,96]{1,0:T(8,128)(2,1)S(1)} %copy-done, bf16[3,2,9]{2,1,0:T(2,128)(2,1)S(1)} %bitcast.4), custom_call_target="tpu_custom_call" | custom-call | flops 1000000 | bytes 1000000 | tf_op jit(solution)/shard_map/tables/pallas_call | solution.py:236
  11.2 4.5 %all-to-all-done.refs_2_ = bf16[8,32,128]{2,1,0:T(8,128)(2,1)S(1)} async-done(((bf16[8,32,128]{2,1,0:T(8,128)(2,1)}), bf16[8,32,128]{2,1,0:T(8,128)(2,1)S(1)}, u32[]{:S(2)}, u32[]{:S(2)}) %all-to-all-start) | async-done | bytes 65568 | tf_op jit(solution)/shard_map/all_to_all | solution.py:294
  15.7 0.0 collective-permute-start
  15.7 1.6 %collective-permute-start.1 = (bf16[8,32,128]{2,1,0:T(8,128)(2,1)S(1)}, bf16[8,32,128]{2,1,0:T(8,128)(2,1)S(1)}, u32[]{:S(2)}, u32[]{:S(2)}) collective-permute-start(bf16[8,32,128]{2,1,0:T(8,128)(2,1)S(1)} %all-to-all-done.refs_2_), channel_id=1, source_target_pairs={{0,8},{8,0},{16,24},{24,16},{1,9},{9,1},{17,25},{25,17},{2,10},{10... | collective-permute-start | bytes 196616 | tf_op jit(solution)/shard_map/ppermute | solution.py:264
  17.3 0.0 collective-permute-done.2.mate_ref
  17.3 0.6 %squares.1.refs_4_ = bf16[2304,256]{1,0:T(8,128)(2,1)S(1)} custom-call(bf16[9,20,80]{2,1,0:T(8,128)(2,1)S(1)} %bitcast.6, bf16[9,20,80]{2,1,0:T(8,128)(2,1)S(1)} %collective-permute-done.2.mate_ref), custom_call_target="tpu_custom_call" | custom-call | flops 20000000000 | bytes 1000000 | tf_op jit(solution)/shard_map/squares/pallas_call | solution.py:236
  17.9 0.0 copy-start.2
  17.9 0.0 copy-start.3
  17.9 0.0 copy-start.6
  17.9 2.1 %collective-permute-done.refs_0_ = bf16[8,32,128]{2,1,0:T(8,128)(2,1)S(1)} collective-permute-done((bf16[8,32,128]{2,1,0:T(8,128)(2,1)S(1)}, bf16[8,32,128]{2,1,0:T(8,128)(2,1)S(1)}, u32[]{:S(2)}, u32[]{:S(2)}) %collective-permute-start) | collective-permute-done | bytes 65568 | tf_op jit(solution)/shard_map/ppermute | solution.py:264
  20.0 0.0 collective-permute-done.1.refs_1_
  20.0 1.0 %conv.1 = (bf16[32,128]{1,0:T(8,128)(2,1)S(1)}, bf16[32,128]{1,0:T(8,128)(2,1)S(1)}, bf16[32,128]{1,0:T(8,128)(2,1)S(1)}, bf16[32,128]{1,0:T(8,128)(2,1)S(1)}) custom-call(bf16[8,32,128]{2,1,0:T(8,128)(2,1)S(1)} %collective-permute-done.refs_0_, bf16[8,32,128]{2,1,0:T(8,128)(2,1)S(1)} %collective-permute-done.1.refs_1_, ...), custom_call_target="tpu_custom_call" | custom-call | flops 10000000000 | bytes 1000000 | tf_op jit(solution)/shard_map/conv/pallas_call | solution.py:236
  21.1 0.6 %collective-permute-start.3 = (bf16[32,128]{1,0:T(8,128)(2,1)S(1)}, bf16[32,128]{1,0:T(8,128)(2,1)S(1)}, u32[]{:S(2)}, u32[]{:S(2)}) collective-permute-start(bf16[32,128]{1,0:T(8,128)(2,1)S(1)} %get-tuple-element.9), channel_id=1, source_target_pairs={{0,6},{1,7},{2,4},{3,5},{4,2},{5,3},{6,0},{7,1},{8,14},{9,15},{10,... | collective-permute-start | bytes 24584 | tf_op jit(solution)/shard_map/ppermute | solution.py:252
  21.7 1.1 %collective-permute-start.4 = (bf16[32,128]{1,0:T(8,128)(2,1)S(1)}, bf16[32,128]{1,0:T(8,128)(2,1)S(1)}, u32[]{:S(2)}, u32[]{:S(2)}) collective-permute-start(bf16[32,128]{1,0:T(8,128)(2,1)S(1)} %get-tuple-element.10), channel_id=1, source_target_pairs={{0,4},{1,5},{2,6},{3,7},{4,0},{5,1},{6,2},{7,3},{8,12},{9,13},{10,... | collective-permute-start | bytes 24584 | tf_op jit(solution)/shard_map/ppermute | solution.py:252
  22.8 2.7 %collective-permute-start.5 = (bf16[32,128]{1,0:T(8,128)(2,1)S(1)}, bf16[32,128]{1,0:T(8,128)(2,1)S(1)}, u32[]{:S(2)}, u32[]{:S(2)}) collective-permute-start(bf16[32,128]{1,0:T(8,128)(2,1)S(1)} %get-tuple-element.11), channel_id=1, source_target_pairs={{0,2},{1,3},{2,0},{3,1},{4,6},{5,7},{6,4},{7,5},{8,10},{9,11},{10,... | collective-permute-start | bytes 24584 | tf_op jit(solution)/shard_map/ppermute | solution.py:252
  25.5 1.1 %collective-permute-done.3.refs_0_ = bf16[32,128]{1,0:T(8,128)(2,1)S(1)} collective-permute-done((bf16[32,128]{1,0:T(8,128)(2,1)S(1)}, bf16[32,128]{1,0:T(8,128)(2,1)S(1)}, u32[]{:S(2)}, u32[]{:S(2)}) %collective-permute-start.3) | collective-permute-done | bytes 8224 | tf_op jit(solution)/shard_map/ppermute | solution.py:252
  26.6 0.0 collective-permute-done.4.refs_1_
  26.6 0.6 %collective-permute-done.5.refs_2_ = bf16[32,128]{1,0:T(8,128)(2,1)S(1)} collective-permute-done((bf16[32,128]{1,0:T(8,128)(2,1)S(1)}, bf16[32,128]{1,0:T(8,128)(2,1)S(1)}, u32[]{:S(2)}, u32[]{:S(2)}) %collective-permute-start.5) | collective-permute-done | bytes 8224 | tf_op jit(solution)/shard_map/ppermute | solution.py:252
  27.2 0.0 copy-done.2
  27.2 0.0 copy-done.3
  27.2 0.0 copy-done.6
  27.2 1.6 %tail.1 = bf16[12,2,640]{2,1,0:T(2,128)(2,1)} custom-call(bf16[32,128]{1,0:T(8,128)(2,1)S(1)} %collective-permute-done.3.refs_0_, bf16[32,128]{1,0:T(8,128)(2,1)S(1)} %collective-permute-done.4.refs_1_, bf16[32,128]{1,0:T(8,128)(2,1)S(1)} %collective-permute-done.5.refs_2_, bf16[32,128]{1,0:T(8,128)(2,1)S(1)} %get-tuple-element.12.refs_3_, ...), custom_call_target="tpu_custom_call" | custom-call | flops 1000000000 | bytes 1000000 | tf_op jit(solution)/shard_map/tail/pallas_call | solution.py:236
Async XLA Ops:
  0.0 0.8 %copy-start.5 = (bf16[2,12,640]{2,0,1:T(2,128)(2,1)S(1)}, bf16[2,12,640]{2,0,1:T(2,128)(2,1)}, u32[]{:S(2)}) copy-start(bf16[2,12,640]{2,0,1:T(2,128)(2,1)} %param.7) | copy-start | bytes 92164
  0.8 8.1 %copy-start.4 = (bf16[9,80,20]{1,2,0:T(8,128)(2,1)S(1)}, bf16[9,80,20]{1,2,0:T(8,128)(2,1)}, u32[]{:S(2)}) copy-start(bf16[9,80,20]{1,2,0:T(8,128)(2,1)} %param.9) | copy-start | bytes 86404
  0.8 10.1 %copy-start = (bf16[9,96]{1,0:T(8,128)(2,1)S(1)}, bf16[9,96]{1,0:T(8,128)(2,1)}, u32[]{:S(2)}) copy-start(bf16[9,96]{1,0:T(8,128)(2,1)} %filter_ref.1) | copy-start | bytes 5188
  0.8 10.1 %copy-start.1 = (bf16[9,2,3]{0,1,2:T(2,128)(2,1)S(1)}, bf16[9,2,3]{0,1,2:T(2,128)(2,1)}, u32[]{:S(2)}) copy-start(bf16[9,2,3]{0,1,2:T(2,128)(2,1)} %param.10) | copy-start | bytes 328
  1.6 14.2 %all-to-all-start = ((bf16[8,32,128]{2,1,0:T(8,128)(2,1)}), bf16[8,32,128]{2,1,0:T(8,128)(2,1)S(1)}, u32[]{:S(2)}, u32[]{:S(2)}) async-start(bf16[8,32,128]{2,1,0:T(8,128)(2,1)} %pack.1), calls=%async_computation | async-start | bytes 131072 | tf_op jit(solution)/shard_map/all_to_all | solution.py:294
  8.8 8.5 %collective-permute-start.2 = (bf16[9,20,80]{2,1,0:T(8,128)(2,1)S(1)}, bf16[9,20,80]{2,1,0:T(8,128)(2,1)S(1)}, u32[]{:S(2)}, u32[]{:S(2)}) collective-permute-start(bf16[9,20,80]{2,1,0:T(8,128)(2,1)S(1)} %bitcast.5), channel_id=1, source_target_pairs={{0,1},{1,0},{2,3},{3,2},{4,5},{5,4},{6,7},{7,6},{8,9},{9,8},{10,11... | collective-permute-start | bytes 86408 | tf_op jit(solution)/shard_map/ppermute | solution.py:257
  15.7 4.3 %collective-permute-start = (bf16[8,32,128]{2,1,0:T(8,128)(2,1)S(1)}, bf16[8,32,128]{2,1,0:T(8,128)(2,1)S(1)}, u32[]{:S(2)}, u32[]{:S(2)}) collective-permute-start(bf16[8,32,128]{2,1,0:T(8,128)(2,1)S(1)} %all-to-all-done.refs_2_), channel_id=1, source_target_pairs={{0,24},{8,16},{16,8},{24,0},{1,25},{9,17},{17,9},{25,1},{2,26},{10... | collective-permute-start | bytes 196616 | tf_op jit(solution)/shard_map/ppermute | solution.py:264
  15.7 4.3 %collective-permute-start.1 = (bf16[8,32,128]{2,1,0:T(8,128)(2,1)S(1)}, bf16[8,32,128]{2,1,0:T(8,128)(2,1)S(1)}, u32[]{:S(2)}, u32[]{:S(2)}) collective-permute-start(bf16[8,32,128]{2,1,0:T(8,128)(2,1)S(1)} %all-to-all-done.refs_2_), channel_id=1, source_target_pairs={{0,8},{8,0},{16,24},{24,16},{1,9},{9,1},{17,25},{25,17},{2,10},{10... | collective-permute-start | bytes 196616 | tf_op jit(solution)/shard_map/ppermute | solution.py:264
  17.9 9.2 %copy-start.2 = (bf16[640,1280]{1,0:T(8,128)(2,1)S(1)}, bf16[640,1280]{1,0:T(8,128)(2,1)}, u32[]{:S(2)}) copy-start(bf16[640,1280]{1,0:T(8,128)(2,1)} %refs_5_.1) | copy-start | bytes 4915204
  17.9 9.2 %copy-start.3 = (bf16[1280,640]{1,0:T(8,128)(2,1)S(1)}, bf16[1280,640]{1,0:T(8,128)(2,1)}, u32[]{:S(2)}) copy-start(bf16[1280,640]{1,0:T(8,128)(2,1)} %refs_6_.1) | copy-start | bytes 4915204
  17.9 9.2 %copy-start.6 = (bf16[2,12,640]{2,0,1:T(2,128)(2,1)S(1)}, bf16[2,12,640]{2,0,1:T(2,128)(2,1)}, u32[]{:S(2)}) copy-start(bf16[2,12,640]{2,0,1:T(2,128)(2,1)} %param.7) | copy-start | bytes 92164
  21.1 5.5 %collective-permute-start.3 = (bf16[32,128]{1,0:T(8,128)(2,1)S(1)}, bf16[32,128]{1,0:T(8,128)(2,1)S(1)}, u32[]{:S(2)}, u32[]{:S(2)}) collective-permute-start(bf16[32,128]{1,0:T(8,128)(2,1)S(1)} %get-tuple-element.9), channel_id=1, source_target_pairs={{0,6},{1,7},{2,4},{3,5},{4,2},{5,3},{6,0},{7,1},{8,14},{9,15},{10,... | collective-permute-start | bytes 24584 | tf_op jit(solution)/shard_map/ppermute | solution.py:252
  21.7 4.9 %collective-permute-start.4 = (bf16[32,128]{1,0:T(8,128)(2,1)S(1)}, bf16[32,128]{1,0:T(8,128)(2,1)S(1)}, u32[]{:S(2)}, u32[]{:S(2)}) collective-permute-start(bf16[32,128]{1,0:T(8,128)(2,1)S(1)} %get-tuple-element.10), channel_id=1, source_target_pairs={{0,4},{1,5},{2,6},{3,7},{4,0},{5,1},{6,2},{7,3},{8,12},{9,13},{10,... | collective-permute-start | bytes 24584 | tf_op jit(solution)/shard_map/ppermute | solution.py:252
  22.8 4.3 %collective-permute-start.5 = (bf16[32,128]{1,0:T(8,128)(2,1)S(1)}, bf16[32,128]{1,0:T(8,128)(2,1)S(1)}, u32[]{:S(2)}, u32[]{:S(2)}) collective-permute-start(bf16[32,128]{1,0:T(8,128)(2,1)S(1)} %get-tuple-element.11), channel_id=1, source_target_pairs={{0,2},{1,3},{2,0},{3,1},{4,6},{5,7},{6,4},{7,5},{8,10},{9,11},{10,... | collective-permute-start | bytes 24584 | tf_op jit(solution)/shard_map/ppermute | solution.py:252
